TPU v7x, 128 devices: a whole 4x4x4 slice. The times are simulated.
128 devices in a mesh: seq: 8 (over y_lo, z), head: 16 (over x, y_hi, core).
Axes of the slice: x: 4, y: 4 (y_hi: 2, y_lo: 2; y = y_hi * 2 + y_lo), z: 4, core: 2. Of those that a mesh axis runs over, the one named last changes fastest.
Arguments:
- tokens: bfloat16 [8, 1280, 3072], P('seq'), may hold values from -6 to 6
- spatial_modulation: float32 [3, 3072], replicated, may hold values from -3 to 3
- spatial_weights_in: bfloat16 [3072, 16, 384], P(None, 'head'), may hold values from -0.6 to 0.6, as said below
- spatial_weights_out: bfloat16 [16, 128, 3072], P('head'), may hold values from -0.5 to 0.5
- temporal_modulation: float32 [3, 3072], replicated, may hold values from -3 to 3
- temporal_weights_in: bfloat16 [3072, 16, 384], P(None, 'head'), may hold values from -0.6 to 0.6, as said below
- temporal_weights_out: bfloat16 [16, 128, 3072], P('head'), may hold values from -0.5 to 0.5
Outputs:
- updated_tokens: bfloat16 [8, 1280, 3072], P(None, ('seq', 'head'))
Inputs may be any that keep to these rules, and one draw needn't show every extreme that they name: `spatial_weights_in`: query, key and value columns of each head, scaled for a fan-in of 3072. `temporal_weights_in`: query, key and value columns of each head, scaled for a fan-in of 3072.
All inputs are finite; a program needn't handle non-finite values.
Results may differ from a plain program's by a relative error of at most 0.034.
Values may be sent and summed in bfloat16 or wider, within the bound.
A program may use at most 128 MiB of HBM per device.

v0:
```python
import jax
import jax.numpy as jnp
from jax import lax
from jax.sharding import PartitionSpec as P


def modulate(rows, modulation):
    values = rows.astype(jnp.float32)
    center = values - jnp.mean(values, axis=-1, keepdims=True)
    spread = jnp.mean(center * center, axis=-1, keepdims=True)
    normed = center * lax.rsqrt(spread + 1e-06)
    return (normed * (1.0 + modulation[1]) + modulation[0]).astype(jnp.bfloat16)


def frame_attention(inputs):
    queries, keys, values = inputs
    score_scale = queries.shape[-1] ** (-0.5)
    scores = jnp.dot(queries, keys.T, preferred_element_type=jnp.float32) * score_scale
    probs = jax.nn.softmax(scores, axis=-1).astype(jnp.bfloat16)
    return jnp.dot(probs, values, preferred_element_type=jnp.float32).astype(jnp.bfloat16)


def shards(
    tokens,
    spatial_modulation,
    spatial_weights_in,
    spatial_weights_out,
    temporal_modulation,
    temporal_weights_in,
    temporal_weights_out,
):
    seq_count = lax.axis_size("seq")
    head_count = lax.axis_size("head")
    head_index = lax.axis_index("head")
    frames_here, cell_count, feature_count = tokens.shape
    head_size = spatial_weights_out.shape[1]
    span_rows = cell_count // (seq_count * head_count)
    normed = modulate(tokens, spatial_modulation)
    joined = jnp.einsum(
        "fsd,dc->fsc", normed, spatial_weights_in[:, 0, :], preferred_element_type=jnp.float32
    ).astype(jnp.bfloat16)
    attended = lax.map(
        frame_attention,
        (
            joined[..., :head_size],
            joined[..., head_size : 2 * head_size],
            joined[..., 2 * head_size :],
        ),
    )
    spatial_outward = spatial_weights_out[0]
    temporal_inward = temporal_weights_in[:, 0, :]
    partial_value = jnp.einsum(
        "fsh,hd->fsd", attended, spatial_outward, preferred_element_type=jnp.float32
    )
    summed = lax.psum(partial_value.astype(jnp.bfloat16), "head").astype(jnp.float32)
    middle = (tokens.astype(jnp.float32) + spatial_modulation[2] * summed).astype(jnp.bfloat16)
    moved = lax.all_to_all(middle, "seq", split_axis=1, concat_axis=0, tiled=True)
    residual = lax.dynamic_slice_in_dim(moved, head_index * span_rows, span_rows, 1)
    temporal_joined = jnp.einsum(
        "fpd,dc->fpc",
        modulate(moved, temporal_modulation),
        temporal_inward,
        preferred_element_type=jnp.float32,
    ).astype(jnp.bfloat16)
    score_scale = head_size ** (-0.5)
    tqueries = temporal_joined[..., :head_size]
    tkeys = temporal_joined[..., head_size : 2 * head_size]
    tvalues = temporal_joined[..., 2 * head_size :]
    tscores = (
        jnp.einsum("fph,gph->pfg", tqueries, tkeys, preferred_element_type=jnp.float32)
        * score_scale
    )
    tprobs = jax.nn.softmax(tscores, axis=-1).astype(jnp.bfloat16)
    tattended = jnp.einsum(
        "pfg,gph->pfh", tprobs, tvalues, preferred_element_type=jnp.float32
    ).astype(jnp.bfloat16)
    temporal_outward = temporal_weights_out[0]
    tsummed = lax.psum_scatter(
        jnp.einsum(
            "pfh,hd->pfd", tattended, temporal_outward, preferred_element_type=jnp.float32
        ).astype(jnp.bfloat16),
        "head",
        scatter_dimension=0,
        tiled=True,
    ).astype(jnp.float32)
    result = residual.astype(jnp.float32) + temporal_modulation[2] * jnp.swapaxes(tsummed, 0, 1)
    return result.astype(jnp.bfloat16)


def solution(mesh):
    placed = (
        P("seq", None, None),
        P(),
        P(None, "head", None),
        P("head", None, None),
        P(),
        P(None, "head", None),
        P("head", None, None),
    )
    return jax.shard_map(
        shards,
        mesh=mesh,
        in_specs=placed,
        out_specs=P(None, ("seq", "head"), None),
        check_vma=False,
    )
```

profile of v0, /device:TPU:0, one launch (start us, length us, event | category | flops | bytes accessed | tf_op | source)
XLA Modules:
  0.0 602.4 jit_solution(10042654416951864080)
XLA Ops:
  6.5 0.0 copy-start
  6.5 0.0 all-reduce.2.cloned.1.call-start
  6.5 0.0 copy-start.3
  6.5 1.0 fusion.51
  7.6 4.7 convert_reduce_fusion
  12.3 0.0 copy-done.3
  12.3 2.2 fusion.5
  14.5 0.0 copy-done
  14.5 4.5 fusion.23
  18.9 0.0 copy-start.7
  18.9 1.0 fusion.52
  20.0 0.0 copy-start.4
  20.0 2.8 copy-done.4
  22.7 1.0 fusion.18
  23.7 0.0 copy-done.7
  23.7 12.5 %fusion.14 = bf16[1,1280,3072]{2,1,0:T(8,128)(2,1)} fusion(f32[1280,1280]{0,1:T(8,128)} %copy-done.4, f32[1280]{0:T(1024)S(1)} %fusion.18, f32[1280]{0:T(1024)S(1)} %get-tuple-element.31, bf16[1,128,3072]{2,1,0:T(8,128)(2,1)S(1)} %copy-done.7, bf16[1,1280,384]{2,1,0:T(8,128)(2,1)S(1)} %fusion.23), kind=kOutput, calls=%fused_computation.21 | convolution fusion | flops 1435074560 | bytes 15548416 | tf_op jit(solution)/shard_map/fsh,hd->fsd/dot_general | solution.py:52
  36.2 0.0 all-reduce.2.cloned.1.call-update
  36.2 192.1 %all-reduce.2.cloned.1.call-done = bf16[1,1280,3072]{2,1,0:T(8,128)(2,1)} async-done(((bf16[1,1280,3072]{2,1,0:T(8,128)(2,1)}), bf16[1,1280,3072]{2,1,0:T(8,128)(2,1)}) %all-reduce.2.cloned.1.call-update) | async-done | bytes 7864336 | tf_op jit(solution)/shard_map/psum | solution.py:55
  228.3 7.0 %fusion.13 = bf16[1,1280,3072]{2,1,0:T(8,128)(2,1)S(1)} fusion(bf16[1,1280,3072]{2,1,0:T(8,128)(2,1)} %param.7, bf16[1,1280,3072]{2,1,0:T(8,128)(2,1)} %all-reduce.2.cloned.1.call-done, f32[3072]{0:T(1024)S(1)} %bitcast.67), kind=kLoop, calls=%fused_computation.18 | loop fusion | flops 19660800 | bytes 23605248 | tf_op jit(solution)/shard_map/convert_element_type | solution.py:56
  235.3 71.9 %copy.44 = bf16[1,1280,3072]{2,0,1:T(2,128)(2,1)} copy(bf16[1,1280,3072]{2,1,0:T(8,128)(2,1)S(1)} %fusion.13) | data formatting | bytes 15728640 | tf_op jit(solution)/shard_map/convert_element_type | solution.py:56
  307.2 0.5 broadcast.83
  307.7 46.7 %reduce.4 = bf16[1280,3072]{1,0:T(8,128)(2,1)} reduce(bf16[1280,1,3072]{2,1,0:T(2,128)(2,1)} %bitcast.63, bf16[]{:T(256)} %broadcast.83), dimensions={1}, to_apply=%bitcast.61.reduce_sub_computation | reduce | bytes 15728642
  354.3 10.7 %reshape.94 = bf16[8,2,245760]{2,1,0:T(2,128)(2,1)} reshape(bf16[1280,3072]{1,0:T(8,128)(2,1)} %reduce.4) | data formatting | bytes 15728640
  365.0 0.0 copy-start.5
  365.0 5.1 all-to-all-start
  370.0 0.0 reduce-scatter.2.cloned.1.call-start
  370.1 0.0 copy-done.5
  370.1 88.8 %all-to-all-done = bf16[8,2,245760]{2,1,0:T(2,128)(2,1)} async-done(((bf16[8,2,245760]{2,1,0:T(2,128)(2,1)}), bf16[8,2,245760]{2,1,0:T(2,128)(2,1)}, u32[]{:S(2)}, u32[]{:S(2)}) %all-to-all-start) | async-done | bytes 7864352 | tf_op jit(solution)/shard_map/all_to_all | solution.py:57
  458.9 12.7 %reshape.95 = bf16[1280,1,3072]{2,1,0:T(2,128)(2,1)} reshape(bf16[8,2,245760]{2,1,0:T(2,128)(2,1)} %all-to-all-done) | data formatting | bytes 15728640
  471.6 7.8 %convert_reduce_fusion.1 = (f32[1280]{0:T(1024)S(1)}, bf16[1,1280,3072]{2,1,0:T(8,128)(2,1)S(1)}) fusion(bf16[1,1280,3072]{2,0,1:T(2,128)(2,1)} %bitcast.64), kind=kLoop, calls=%fused_computation.5 | loop fusion | flops 7863040 | bytes 15733760 | tf_op jit(solution)/shard_map/reduce_sum | solution.py:9
  479.5 0.0 copy-start.2
  479.5 2.2 fusion.9
  481.7 0.0 copy-start.6
  481.7 4.7 fusion.12
  486.4 0.0 copy-done.2
  486.4 0.0 copy-done.6
  486.5 4.3 fusion.30
  490.8 0.2 fusion.49
  490.9 0.3 convolution_multiply_fusion.1
  491.3 0.6 fusion.53
  491.9 0.0 copy-start.1
  491.9 6.4 %convolution_convert_fusion.1 = bf16[160,8,3072]{2,1,0:T(8,128)(2,1)} fusion(bf16[1,128,3072]{2,1,0:T(8,128)(2,1)} %param.13, bf16[8,160,128]{2,1,0:T(8,128)(2,1)S(1)} %get-tuple-element.22, f32[160,8]{1,0:T(8,128)S(1)} %fusion.53, f32[160,8,8]{1,2,0:T(8,128)S(1)} %convolution_multiply_fusion.1), kind=kOutput, calls=%fused_computation.26 | convolution fusion | flops 1013382400 | bytes 9024512 | tf_op jit(solution)/shard_map/pfh,hd->pfd/dot_general | solution.py:79
  498.4 0.0 reduce-scatter.2.cloned.1.call-update
  498.4 1.5 constant_dynamic-slice_fusion
  499.9 93.5 %reduce-scatter.2.cloned.1.call-done = bf16[10,8,3072]{2,1,0:T(8,128)(2,1)} async-done(((bf16[160,8,3072]{2,1,0:T(8,128)(2,1)}), bf16[10,8,3072]{2,1,0:T(8,128)(2,1)}) %reduce-scatter.2.cloned.1.call-update) | async-done | bytes 491536 | tf_op jit(solution)/shard_map/reduce_scatter | solution.py:78
  593.4 2.1 fusion.35
  595.6 0.0 copy-done.1
  (5 shorter events, 0.1 us)
Async XLA Ops:
  6.5 7.9 %copy-start = (bf16[3072,1,384]{2,0,1:T(8,128)(2,1)S(1)}, bf16[3072,1,384]{2,0,1:T(8,128)(2,1)}, u32[]{:S(2)}) copy-start(bf16[3072,1,384]{2,0,1:T(8,128)(2,1)} %param.9) | copy-start | bytes 7077892
  6.5 221.8 %all-reduce.2.cloned.1.call-start = ((), (), s32[]{:S(2)}) async-start(), calls=%async_computation.2 | async-start | bytes 15728640 | tf_op jit(solution)/shard_map/psum | solution.py:55
  6.5 5.7 copy-start.3
  18.9 4.8 copy-start.7
  20.0 2.8 copy-start.4
  365.0 5.1 copy-start.5
  365.0 93.9 %all-to-all-start = ((bf16[8,2,245760]{2,1,0:T(2,128)(2,1)}), bf16[8,2,245760]{2,1,0:T(2,128)(2,1)}, u32[]{:S(2)}, u32[]{:S(2)}) async-start(bf16[8,2,245760]{2,1,0:T(2,128)(2,1)} %reshape.94), calls=%async_computation | async-start | bytes 15728640 | tf_op jit(solution)/shard_map/all_to_all | solution.py:57
  370.0 223.4 %reduce-scatter.2.cloned.1.call-start = ((), (), s32[]{:S(2)}) async-start(), calls=%async_computation.3 | async-start | bytes 8355840 | tf_op jit(solution)/shard_map/reduce_scatter | solution.py:78
  479.5 7.0 %copy-start.2 = (bf16[1,1280,3072]{2,1,0:T(8,128)(2,1)}, bf16[1,1280,3072]{2,1,0:T(8,128)(2,1)S(1)}, u32[]{:S(2)}) copy-start(bf16[1,1280,3072]{2,1,0:T(8,128)(2,1)S(1)} %get-tuple-element.14) | copy-start | bytes 23592964
  481.7 4.8 copy-start.6
  491.9 103.7 %copy-start.1 = (bf16[3072,1,384]{2,0,1:T(8,128)(2,1)S(1)}, bf16[3072,1,384]{2,0,1:T(8,128)(2,1)}, u32[]{:S(2)}) copy-start(bf16[3072,1,384]{2,0,1:T(8,128)(2,1)} %param.9) | copy-start | bytes 7077892
Sparse Core Ops, SparseCore 0:
  36.4 191.9 all-reduce.1
  498.5 94.8 reduce-scatter.1
where the time goes:
time: 603 us; the launch traced here: 602 us
  waiting for transfers between devices  374 us (62%)
  local copies, waits for them, and re-layouts  100 us (17%)
  other arithmetic  79.4 us (13%)
  matrix products  29.7 us (5%)
  between operations  13.6 us (2%)
    psum x1, waiting for transfers between devices, shards(): lax.psum(partial_value.astype(jnp.bfloat16), 'head').astype(jnp.float32)  192 us
    reduce_scatter x1, waiting for transfers between devices, shards(): lax.psum_scatter(jnp.einsum('pfh,hd->pfd', tattended, temporal_outward, p...  93.5 us
    all_to_all x1, waiting for transfers between devices, shards(): lax.all_to_all(middle, 'seq', split_axis=1, concat_axis=0, tiled=True)  88.8 us
    convert_element_type x1, local copies, waits for them, and re-layouts, shards(): (tokens.astype(jnp.float32) + spatial_modulation[2] * summed).astype(jnp....  71.9 us
    unnamed x1, other arithmetic  46.7 us
    unnamed x19, local copies, waits for them, and re-layouts  26.7 us
    reduce_sum x2, other arithmetic, modulate(): center = values - jnp.mean(values, axis=-1, keepdims=True)  12.5 us
    dot_general x1, matrix products, shards(): jnp.einsum('fsh,hd->fsd', attended, spatial_outward, preferred_element_ty...  12.5 us
  transfers between devices with their start and end apart: 3, of which 3 were waited for; matrix products, arithmetic and copies ran while one was open for 0% of the time, Pallas kernels for 0%

commit v1 on v0

v1 whole, which is shorter than its diff:
```python
import functools

import jax
import jax.numpy as jnp
from jax import lax
from jax.experimental import pallas as pl
from jax.experimental.pallas import tpu as pltpu
from jax.sharding import PartitionSpec as P

BF = jnp.bfloat16
F32 = jnp.float32
MESH = pl.DeviceIdType.MESH
BLOCKS = 6
LOG2E = 1.4426950408889634


def dot(a, b):
    return jnp.dot(a, b, preferred_element_type=F32)


def dot_nt(a, b):
    return lax.dot_general(a, b, (((1,), (1,)), ((), ())), preferred_element_type=F32)


def iota(shape, axis):
    return lax.broadcasted_iota(jnp.int32, shape, axis)


def floor_div(v, n):
    return jnp.floor((v + 0.5) * (1.0 / n))


def remote(src, dst, send, recv, device):
    return pltpu.make_async_remote_copy(
        src_ref=src, dst_ref=dst, send_sem=send, recv_sem=recv,
        device_id=device, device_id_type=MESH,
    )


def query_rows(quarter, rows, cells):
    r = iota((rows, 1), 0).astype(F32)
    xx = floor_div(r, 80)
    r = r - xx * 80
    ss = floor_div(r, 10)
    ii = r - ss * 10
    p = ss * 160 + xx * 40 + ii + (quarter * 10).astype(F32)
    c = iota((1, cells), 1).astype(F32)
    return jnp.where(p == c, 1.0, 0.0).astype(BF)


def kernel(
    tok_in, smod, win_in, wo_in, tmod, wt_in, wto_in,
    out,
    tok, wi, wx, qb, kb, vx, att, cat, own_rows, wo, wt, wto,
    part, relay, got, shuf, shufr, gath, tnorm, qkv, tatt, part2, relay2, got2, res,
    local_sem, tok_sem, out_sem, win_sem, wsend, wrecv, asend, arecv,
    rsend, rrecv, ssend, srecv, gsend, grecv, rsend2, rrecv2,
):
    d = tok.shape[-1]
    nb = BLOCKS
    cb = d // nb
    hb = cb // 2
    s = lax.axis_index("seq")
    h = lax.axis_index("head")
    yl, z = s // 4, s % 4
    x, q = h // 4, h % 4
    yh, core = q // 2, q % 2
    right = (s, ((x + 1) % 4) * 4 + q)
    left = (s, ((x + 3) % 4) * 4 + q)
    quad = [None] + [
        (s, x * 4 + ((yh + r // 2) % 2) * 2 + (core + r) % 2) for r in (1, 2, 3)
    ]
    mate = quad[1]
    cross = ((1 - yl) * 4 + z, x * 4 + (1 - yh) * 2 + core)
    up = (yl * 4 + (z + 1) % 4, h)
    down = (yl * 4 + (z + 3) % 4, h)
    xr, xl, xo = (x + 1) % 4, (x + 3) % 4, (x + 2) % 4
    zu, zd, zo = (z + 1) % 4, (z + 3) % 4, (z + 2) % 4

    barrier = pltpu.get_barrier_semaphore()
    partners = [right, left] + quad[1:] + [cross] + [((s + j) % 8, h) for j in range(1, 8)]
    for device in partners:
        pl.semaphore_signal(barrier, inc=1, device_id=device, device_id_type=MESH)

    load_w = pltpu.make_async_copy(win_in, wi, win_sem)
    load_w.start()
    loads = [pltpu.make_async_copy(tok_in.at[i], tok.at[i], tok_sem.at[i]) for i in range(4)]
    for load in loads:
        load.start()
    own_loads = [
        pltpu.make_async_copy(src, dst.at[0], local_sem.at[i])
        for i, (src, dst) in enumerate(((wo_in, wo), (wt_in, wt), (wto_in, wto)))
    ]
    for load in own_loads:
        load.start()
    sends = []

    def go(copy):
        copy.start()
        sends.append(copy)
        return copy

    def weight_begin(w, src, buf):
        go(remote(src, buf.at[1], wsend.at[w, 0], wrecv.at[w, 0], mate))
        go(remote(src.at[z], buf.at[2, z], wsend.at[w, 1], wrecv.at[w, 1], cross))

    def weight_a(w, buf):
        piece = buf.at[2, z]
        remote(piece, piece, wsend.at[w, 1], wrecv.at[w, 1], cross).wait_recv()
        go(remote(piece, piece, wsend.at[w, 2], wrecv.at[w, 2], up))
        go(remote(piece, piece, wsend.at[w, 3], wrecv.at[w, 3], down))
        go(remote(piece, buf.at[3, z], wsend.at[w, 4], wrecv.at[w, 4], mate))

    def weight_b(w, buf):
        below, above = buf.at[2, zd], buf.at[2, zu]
        remote(below, below, wsend.at[w, 2], wrecv.at[w, 2], up).wait_recv()
        go(remote(below.at[0], below.at[0], wsend.at[w, 5], wrecv.at[w, 5], up))
        go(remote(below, buf.at[3, zd], wsend.at[w, 7], wrecv.at[w, 7], mate))
        remote(above, above, wsend.at[w, 3], wrecv.at[w, 3], down).wait_recv()
        go(remote(above.at[1], above.at[1], wsend.at[w, 6], wrecv.at[w, 6], down))
        go(remote(above, buf.at[3, zu], wsend.at[w, 8], wrecv.at[w, 8], mate))

    def weight_c(w, buf):
        far = buf.at[2, zo]
        remote(far.at[0], far.at[0], wsend.at[w, 5], wrecv.at[w, 5], up).wait_recv()
        go(remote(far.at[0], buf.at[3, zo, 0], wsend.at[w, 9], wrecv.at[w, 9], mate))
        remote(far.at[1], far.at[1], wsend.at[w, 6], wrecv.at[w, 6], down).wait_recv()
        go(remote(far.at[1], buf.at[3, zo, 1], wsend.at[w, 10], wrecv.at[w, 10], mate))

    def weight_end(w, src, buf):
        own_loads[w].wait()
        remote(src, buf.at[1], wsend.at[w, 0], wrecv.at[w, 0], mate).wait_recv()
        for k, piece in ((4, buf.at[3, z]), (7, buf.at[3, zd]), (8, buf.at[3, zu]),
                         (9, buf.at[3, zo, 0]), (10, buf.at[3, zo, 1])):
            remote(piece, piece, wsend.at[w, k], wrecv.at[w, k], mate).wait_recv()

    load_w.wait()
    m0 = smod[0:1, :]
    m0_high = m0.astype(BF).astype(F32)
    row = iota((16, d), 0)
    shift_rows = jnp.where(row == 0, m0_high, jnp.where(row == 1, m0 - m0_high, 0.0)).astype(BF)
    bias = jnp.sum(dot(shift_rows, wi[...]), axis=0, keepdims=True)

    def fold(i, _):
        rows = pl.ds(pl.multiple_of(i * 128, 128), 128)
        gain = jnp.broadcast_to(1.0 + smod[1:2, rows], (128, 128)).T
        for j in range(3):
            cols = slice(j * 128, (j + 1) * 128)
            wx[rows, cols] = (wi[rows, cols].astype(F32) * gain).astype(BF)
        wx[rows, 384:512] = jnp.ones((128, 128), BF)
        return 0

    lax.fori_loop(0, d // 128, fold, 0, unroll=4)
    colsum = dot(jnp.ones((16, d), BF), wx[:, 0:384])[0:1, :]

    pl.semaphore_wait(barrier, len(partners))
    weight_begin(0, wo_in, wo)
    weight_begin(1, wt_in, wt)

    def project(i, _):
        pltpu.make_async_copy(tok_in.at[i], tok.at[i], tok_sem.at[i]).wait()
        t = tok[i]
        raw = dot(t, wx[...])
        base = t[:, 0:1].astype(F32)
        squares = jnp.zeros((320, 128), F32)
        for j in range(d // 128):
            e = t[:, j * 128:(j + 1) * 128].astype(F32) - base
            squares = squares + e * e
        mean = raw[:, 384:385] * (1.0 / d)
        spread = jnp.sum(squares, axis=1, keepdims=True) * (1.0 / d) - (mean - base) * (mean - base)
        scale = lax.rsqrt(spread + 1e-06)
        full = ((raw[:, 0:384] - mean * colsum) * scale + bias).astype(BF)
        rows = pl.ds(pl.multiple_of(i * 320, 320), 320)
        qb[rows, :] = full[:, 0:128]
        kb[rows, :] = full[:, 128:256]
        vx[rows, 0:128] = full[:, 256:384]
        vx[rows, 128:256] = jnp.ones((320, 128), BF)
        return 0

    lax.fori_loop(0, 4, project, 0)
    weight_a(0, wo)

    score_scale = 128 ** (-0.5) * LOG2E

    def attend(r):
        quarter = ((yh + r // 2) % 2) * 2 + (core + r) % 2
        pick = query_rows(quarter, 320, 1280)
        queries = dot(pick, qb[...]).astype(BF)
        scores = dot_nt(queries, kb[...])
        top = jnp.max(scores, axis=1, keepdims=True)
        probs = jnp.exp2((scores - top) * score_scale).astype(BF)
        both = dot(probs, vx[...])
        result = (both[:, 0:128] / both[:, 128:256]).astype(BF)
        if r:
            att[r] = result
            go(remote(att.at[r], cat.at[r], asend.at[r], arecv.at[r], quad[r]))
        else:
            cat[0] = result

    attend(3)
    attend(2)
    weight_b(0, wo)
    attend(1)
    attend(0)
    weight_c(0, wo)

    first = h * 10
    start = jnp.minimum((first // 16) * 16, 128)
    skip = first - start
    r80 = iota((80, 1), 0).astype(F32)
    s80 = floor_div(r80, 10)
    target = s80 * 32 + (r80 - s80 * 10) + skip.astype(F32)
    pick_own = jnp.where(target == iota((1, 256), 1).astype(F32), 1.0, 0.0).astype(BF)
    flat = tok.reshape(1280, d)
    windows = jnp.concatenate(
        [flat[pl.ds(pl.multiple_of(k * 160 + start, 16), 32), :] for k in range(8)], axis=0
    )
    own_rows[...] = dot(pick_own, windows).astype(BF)

    t128 = iota((128, 1), 0).astype(F32)
    blk = floor_div(t128, 16)
    pos = t128 - blk * 16
    col80 = iota((1, 80), 1).astype(F32)
    spread_rows = jnp.where((pos < 10) & (blk * 10 + pos == col80), 1.0, 0.0).astype(BF)
    i80 = floor_div(r80, 8)
    f80 = r80 - i80 * 8
    dense_rows = jnp.where(f80 * 16 + i80 == iota((1, 128), 1).astype(F32), 1.0, 0.0).astype(BF)

    def ring_compute(b, lhs, w, buf):
        cols = pl.ds(b * cb, cb)
        block = w[:, :, :, :, cols].reshape(512, cb)
        buf[b] = dot(lhs, block).astype(BF).reshape(4, 80, cb)

    def ring_first(b, buf, rel, rec, ss, rs):
        lo, hi = pl.ds(0, hb), pl.ds(hb, hb)
        go(remote(buf.at[b, xo, :, lo], rel.at[b, 0], ss.at[b, 0], rs.at[b, 0], right))
        go(remote(buf.at[b, xo, :, hi], rel.at[b, 1], ss.at[b, 1], rs.at[b, 1], left))
        go(remote(buf.at[b, xr, :, hi], rec.at[b, 0, 1], ss.at[b, 2], rs.at[b, 2], right))
        go(remote(buf.at[b, xl, :, lo], rec.at[b, 1, 0], ss.at[b, 3], rs.at[b, 3], left))

    def ring_second(b, buf, rel, rec, ss, rs):
        lo, hi = pl.ds(0, hb), pl.ds(hb, hb)
        remote(rel.at[b, 0], rel.at[b, 0], ss.at[b, 0], rs.at[b, 0], right).wait_recv()
        rel[b, 0] = (rel[b, 0].astype(F32) + buf[b, xr, :, lo].astype(F32)).astype(BF)
        go(remote(rel.at[b, 0], rec.at[b, 0, 0], ss.at[b, 4], rs.at[b, 4], right))
        remote(rel.at[b, 1], rel.at[b, 1], ss.at[b, 1], rs.at[b, 1], left).wait_recv()
        rel[b, 1] = (rel[b, 1].astype(F32) + buf[b, xl, :, hi].astype(F32)).astype(BF)
        go(remote(rel.at[b, 1], rec.at[b, 1, 1], ss.at[b, 5], rs.at[b, 5], left))

    def ring_last(b, buf, rec, ss, rs):
        for k, (side, half) in ((2, (0, 1)), (3, (1, 0)), (4, (0, 0)), (5, (1, 1))):
            remote(rec.at[b, side, half], rec.at[b, side, half], ss.at[b, k], rs.at[b, k], right).wait_recv()
        own = buf[b, x].astype(F32)
        halves = [
            own[:, k * hb:(k + 1) * hb] + rec[b, 0, k].astype(F32) + rec[b, 1, k].astype(F32)
            for k in range(2)
        ]
        return jnp.concatenate(halves, axis=1)

    def swap_send(b):
        total = ring_last(b, part, got, rsend, rrecv)
        cols = pl.ds(b * cb, cb)
        middle = (own_rows[:, cols].astype(F32) + smod[2:3, cols] * total).astype(BF)
        padded = dot(spread_rows, middle).astype(BF).reshape(8, 16, cb)
        shuf[b] = padded
        for j in range(1, 8):
            to = (s + j) % 8
            go(remote(shuf.at[b, to], shufr.at[b, s], ssend.at[b, j], srecv.at[b, j], (to, h)))
        shufr[b, s] = shuf[b, s]

    def gather_send(b):
        for j in range(1, 8):
            piece = shufr.at[b, (s + 8 - j) % 8]
            remote(piece, piece, ssend.at[b, j], srecv.at[b, j], right).wait_recv()
        gath[b, x] = dot(dense_rows, shufr[b].reshape(128, cb)).astype(BF)
        mine = gath.at[b, x]
        go(remote(mine, mine, gsend.at[b, 0], grecv.at[b, 0], right))
        go(remote(mine, mine, gsend.at[b, 1], grecv.at[b, 1], left))

    def gather_relay(b):
        from_left, from_right = gath.at[b, xl], gath.at[b, xr]
        remote(from_left, from_left, gsend.at[b, 0], grecv.at[b, 0], right).wait_recv()
        piece = gath.at[b, xl, :, pl.ds(0, hb)]
        go(remote(piece, piece, gsend.at[b, 2], grecv.at[b, 2], right))
        remote(from_right, from_right, gsend.at[b, 1], grecv.at[b, 1], left).wait_recv()
        piece = gath.at[b, xr, :, pl.ds(hb, hb)]
        go(remote(piece, piece, gsend.at[b, 3], grecv.at[b, 3], left))

    def gather_end(b):
        lo, hi = gath.at[b, xo, :, pl.ds(0, hb)], gath.at[b, xo, :, pl.ds(hb, hb)]
        remote(lo, lo, gsend.at[b, 2], grecv.at[b, 2], right).wait_recv()
        remote(hi, hi, gsend.at[b, 3], grecv.at[b, 3], left).wait_recv()

    for r in (1, 2, 3):
        remote(att.at[r], cat.at[r], asend.at[r], arecv.at[r], quad[r]).wait_recv()
    weight_end(0, wo_in, wo)
    lhs = jnp.concatenate([cat[r] for r in range(4)], axis=1)

    for t in range(nb + 5):
        if t < nb:
            ring_compute(t, lhs, wo, part)
            ring_first(t, part, relay, got, rsend, rrecv)
        if 0 <= t - 1 < nb:
            ring_second(t - 1, part, relay, got, rsend, rrecv)
        if t == 1:
            weight_begin(2, wto_in, wto)
            weight_a(1, wt)
        if 0 <= t - 2 < nb:
            swap_send(t - 2)
        if 0 <= t - 3 < nb:
            gather_send(t - 3)
        if t == 4:
            weight_b(1, wt)
        if 0 <= t - 4 < nb:
            gather_relay(t - 4)
        if t == nb:
            weight_c(1, wt)
        if 0 <= t - 5 < nb:
            gather_end(t - 5)

    weight_a(2, wto)
    total = jnp.zeros((320, 128), F32)
    squares = jnp.zeros((320, 128), F32)
    base = gath[0, :, :, 0:128].reshape(320, 128)[:, 0:1].astype(F32)
    for b in range(nb):
        rows = gath[b].reshape(320, cb)
        for j in range(cb // 128):
            e = rows[:, j * 128:(j + 1) * 128].astype(F32) - base
            total = total + e
            squares = squares + e * e
    off = jnp.sum(total, axis=1, keepdims=True) * (1.0 / d)
    spread = jnp.sum(squares, axis=1, keepdims=True) * (1.0 / d) - off * off
    scale = lax.rsqrt(spread + 1e-06)
    mean = base + off
    for b in range(nb):
        cols = slice(b * cb, (b + 1) * cb)
        rows = gath[b].reshape(320, cb).astype(F32)
        tnorm[:, cols] = ((rows - mean) * scale * (1.0 + tmod[1:2, cols]) + tmod[0:1, cols]).astype(BF)
    weight_b(2, wto)
    weight_end(1, wt_in, wt)

    def temporal_project(j, _):
        qkv[j] = dot(tnorm[...], wt[j].reshape(d, 384)).astype(BF)
        return 0

    lax.fori_loop(0, 4, temporal_project, 0)
    weight_c(2, wto)
    same = (iota((320, 320), 0) >> 3) == (iota((320, 320), 1) >> 3)
    for j in range(4):
        scores = dot_nt(qkv[j, :, 0:128], qkv[j, :, 128:256])
        scores = jnp.where(same, scores, -1e30)
        top = jnp.max(scores, axis=1, keepdims=True)
        probs = jnp.exp2((scores - top) * score_scale)
        probs = (probs / jnp.sum(probs, axis=1, keepdims=True)).astype(BF)
        tatt[:, j * 128:(j + 1) * 128] = dot(probs, qkv[j, :, 256:384]).astype(BF)
    weight_end(2, wto_in, wto)
    lhs = tatt[...]

    stores = []
    for t in range(nb + 2):
        if t < nb:
            ring_compute(t, lhs, wto, part2)
            ring_first(t, part2, relay2, got2, rsend2, rrecv2)
        if 0 <= t - 1 < nb:
            ring_second(t - 1, part2, relay2, got2, rsend2, rrecv2)
        if 0 <= t - 2 < nb:
            b = t - 2
            total = ring_last(b, part2, got2, rsend2, rrecv2)
            cols = pl.ds(b * cb, cb)
            res[b] = (gath[b, x].astype(F32) + tmod[2:3, cols] * total).astype(BF)
            store = pltpu.make_async_copy(res.at[b], out.at[:, cols], out_sem.at[b])
            store.start()
            stores.append(store)
    for store in stores:
        store.wait()
    for copy in sends:
        copy.wait_send()


def shards(
    tokens, spatial_modulation, spatial_weights_in, spatial_weights_out,
    temporal_modulation, temporal_weights_in, temporal_weights_out,
):
    d = tokens.shape[-1]
    nb, cb = BLOCKS, d // BLOCKS
    hb = cb // 2
    dma = pltpu.SemaphoreType.DMA
    any_space = pl.BlockSpec(memory_space=pl.ANY)
    vmem = pl.BlockSpec(memory_space=pltpu.VMEM)
    out_weights = pltpu.VMEM((4, 4, 2, 16, d), BF)
    ring = [
        pltpu.VMEM((nb, 4, 80, cb), BF),
        pltpu.VMEM((nb, 2, 80, hb), BF),
        pltpu.VMEM((nb, 2, 2, 80, hb), BF),
    ]
    result = pl.pallas_call(
        kernel,
        out_shape=jax.ShapeDtypeStruct((80, d), BF),
        in_specs=[any_space, vmem, any_space, any_space, vmem, any_space, any_space],
        out_specs=any_space,
        scratch_shapes=[
            pltpu.VMEM((4, 320, d), BF),
            pltpu.VMEM((d, 384), BF),
            pltpu.VMEM((d, 512), BF),
            pltpu.VMEM((1280, 128), BF),
            pltpu.VMEM((1280, 128), BF),
            pltpu.VMEM((1280, 256), BF),
            pltpu.VMEM((4, 320, 128), BF),
            pltpu.VMEM((4, 320, 128), BF),
            pltpu.VMEM((80, d), BF),
            out_weights,
            pltpu.VMEM((4, 4, 2, d // 8, 384), BF),
            out_weights,
            *ring,
            pltpu.VMEM((nb, 8, 16, cb), BF),
            pltpu.VMEM((nb, 8, 16, cb), BF),
            pltpu.VMEM((nb, 4, 80, cb), BF),
            pltpu.VMEM((320, d), BF),
            pltpu.VMEM((4, 320, 384), BF),
            pltpu.VMEM((320, 512), BF),
            *ring,
            pltpu.VMEM((nb, 80, cb), BF),
            dma((3,)), dma((4,)), dma((nb,)), dma(()),
            dma((3, 11)), dma((3, 11)),
            dma((4,)), dma((4,)),
            dma((nb, 6)), dma((nb, 6)),
            dma((nb, 8)), dma((nb, 8)),
            dma((nb, 4)), dma((nb, 4)),
            dma((nb, 6)), dma((nb, 6)),
        ],
        compiler_params=pltpu.CompilerParams(
            collective_id=0, has_side_effects=True, vmem_limit_bytes=60 * 1024 * 1024
        ),
        cost_estimate=pl.CostEstimate(
            flops=9_000_000_000, bytes_accessed=16_000_000, transcendentals=2_000_000
        ),
    )(
        tokens.reshape(4, 320, d),
        spatial_modulation,
        jnp.transpose(spatial_weights_in, (1, 0, 2)).reshape(d, 384),
        spatial_weights_out.reshape(4, 2, 16, d),
        temporal_modulation,
        jnp.transpose(temporal_weights_in, (1, 0, 2)).reshape(4, 2, d // 8, 384),
        temporal_weights_out.reshape(4, 2, 16, d),
    )
    return jnp.transpose(result.reshape(10, 8, d), (1, 0, 2))


def solution(mesh):
    placed = (
        P("seq", None, None),
        P(),
        P(None, "head", None),
        P("head", None, None),
        P(),
        P(None, "head", None),
        P("head", None, None),
    )
    return jax.shard_map(
        shards,
        mesh=mesh,
        in_specs=placed,
        out_specs=P(None, ("seq", "head"), None),
        check_vma=False,
    )
```

time: 603 us -> 121 us (0.20)
  waiting for transfers between devices: 374 us -> 0 us
  Pallas kernels: 0 us -> 119 us
  local copies, waits for them, and re-layouts: 100 us -> 1.84 us
  other arithmetic: 79.4 us -> 0 us
  matrix products: 29.7 us -> 0 us
  between operations: 13.6 us -> 0.01 us
    psum x1 -> x0, waiting for transfers between devices: 192 us -> none  [shards(): lax.psum(partial_value.astype(jnp.bfloat16), 'head').astype(jnp.float32)]
    pallas_call x0 -> x1, Pallas kernels: none -> 119 us  [shards(): pl.pallas_call(kernel, out_shape=jax.ShapeDtypeStruct((80, d), BF), in_sp...]
    reduce_scatter x1 -> x0, waiting for transfers between devices: 93.5 us -> none  [shards(): lax.psum_scatter(jnp.einsum('pfh,hd->pfd', tattended, temporal_outward, p...]
    all_to_all x1 -> x0, waiting for transfers between devices: 88.8 us -> none  [shards(): lax.all_to_all(middle, 'seq', split_axis=1, concat_axis=0, tiled=True)]
    convert_element_type x1 -> x0, local copies, waits for them, and re-layouts: 71.9 us -> none  [shards(): (tokens.astype(jnp.float32) + spatial_modulation[2] * summed).astype(jnp....]
    unnamed x1 -> x0, other arithmetic: 46.7 us -> none
    dot_general x6 -> x0, matrix products: 29.1 us -> none  [the longest x1 12.5 us: shards(): jnp.einsum('fsh,hd->fsd', attended, spatial_outward, preferred_element_ty...]
    unnamed x19 -> x1, local copies, waits for them, and re-layouts: 26.7 us -> 1.84 us
  transfers between devices with their start and end apart: 3 -> 0, of which waited for: 3 -> 0; matrix products, arithmetic and copies ran while one was open for 0% -> 0% of each run, Pallas kernels for 0% -> 0%
where the time goes in v1:
time: 121 us; the launch traced here: 120 us
  Pallas kernels  119 us (98%)
  local copies, waits for them, and re-layouts  1.84 us (2%)
    pallas_call x1, Pallas kernels, shards(): pl.pallas_call(kernel, out_shape=jax.ShapeDtypeStruct((80, d), BF), in_sp...  119 us

profile of v1, /device:TPU:0, one launch (start us, length us, event | category | flops | bytes accessed | tf_op | source)
XLA Modules:
  0.0 120.5 jit_solution(14645263010016061002)
XLA Ops:
  0.0 118.6 %shard_map.73 = bf16[80,3072]{1,0:T(8,128)(2,1)} custom-call(bf16[4,320,3072]{2,1,0:T(8,128)(2,1)} %bitcast.9, f32[3,3072]{1,0:T(4,128)} %smod.1, bf16[3072,384]{1,0:T(8,128)(2,1)} %bitcast.10, bf16[4,2,16,3072]{3,2,1,0:T(8,128)(2,1)} %bitcast.12, f32[3,3072]{1,0:T(4,128)} %tmod.1, bf16[4,2,384,384]{3,2,1,0:T(8,128)(2,1)} %bitcast.11, ...), custom_call_target="tpu_custom_call" | custom-call | flops 8999999488 | bytes 16000000 | tf_op jit(solution)/shard_map/pallas_call | solution.py:396
  118.6 1.8 %copy.9 = bf16[8,10,3072]{2,0,1:T(8,128)(2,1)} copy(bf16[8,10,3072]{2,0,1:T(8,128)(2,1)} %bitcast.8) | data formatting | bytes 983040

commit v2 on v1

v2 whole, which is shorter than its diff:
```python
import functools

import jax
import jax.numpy as jnp
from jax import lax
from jax.experimental import pallas as pl
from jax.experimental.pallas import tpu as pltpu
from jax.sharding import PartitionSpec as P

BF = jnp.bfloat16
F32 = jnp.float32
MESH = pl.DeviceIdType.MESH
BLOCKS = 5
LOG2E = 1.4426950408889634
TICKS = (
    (0, (1, 0)), (0, (1, 1)), (1, (1, 2)), (1, (1, 3)), (2, (1,)), (3, (2, 0)), (3, (2, 1)), (4, (2,)),
)


def dot(a, b):
    return jnp.dot(a, b, preferred_element_type=F32)


def dot_nt(a, b):
    return lax.dot_general(a, b, (((1,), (1,)), ((), ())), preferred_element_type=F32)


def iota(shape, axis):
    return lax.broadcasted_iota(jnp.int32, shape, axis)


def one_hot(hit):
    return jnp.where(hit, 1.0, 0.0).astype(BF)


def remote(src, dst, send, recv, device):
    return pltpu.make_async_remote_copy(
        src_ref=src, dst_ref=dst, send_sem=send, recv_sem=recv,
        device_id=device, device_id_type=MESH,
    )


def kernel(
    tok_in, smod, win_in, wo_in, tmod, wt_in, wto_in,
    out,
    tok, wi, wx, qb, kb, vx, att, cat, own_rows, wo, wt, wto,
    part, relay, got, shuf, shufr, gath, part2, relay2, got2, res,
    local_sem, tok_sem, out_sem, win_sem, wsend, wrecv, asend, arecv,
    rsend, rrecv, ssend, srecv, gsend, grecv, rsend2, rrecv2,
):
    d = tok.shape[-1]
    nb = BLOCKS
    hb = d // 2
    eighth = d // 8
    s = lax.axis_index("seq")
    h = lax.axis_index("head")
    yl, z = s // 4, s % 4
    x, q = h // 4, h % 4
    yh, core = q // 2, q % 2
    right = (s, ((x + 1) % 4) * 4 + q)
    left = (s, ((x + 3) % 4) * 4 + q)
    quarters = [((yh + r // 2) % 2) * 2 + (core + r) % 2 for r in range(4)]
    quad = [(s, x * 4 + k) for k in quarters]
    mate = quad[1]
    cross = ((1 - yl) * 4 + z, x * 4 + (1 - yh) * 2 + core)
    beside = ((1 - yl) * 4 + z, h)
    up = (yl * 4 + (z + 1) % 4, h)
    down = (yl * 4 + (z + 3) % 4, h)
    xr, xl, xo = (x + 1) % 4, (x + 3) % 4, (x + 2) % 4
    zu, zd, zo = (z + 1) % 4, (z + 3) % 4, (z + 2) % 4

    barrier = pltpu.get_barrier_semaphore()
    partners = [right, left] + quad[1:] + [cross] + [((s + j) % 8, h) for j in range(1, 8)]
    for device in partners:
        pl.semaphore_signal(barrier, inc=1, device_id=device, device_id_type=MESH)

    load_w = pltpu.make_async_copy(win_in, wi, win_sem)
    load_w.start()
    for i in range(4):
        pltpu.make_async_copy(tok_in.at[i], tok.at[i], tok_sem.at[i]).start()
    weights = ((wo_in, wo), (wt_in, wt), (wto_in, wto))
    own_loads = [
        pltpu.make_async_copy(src, dst.at[0], local_sem.at[i]) for i, (src, dst) in enumerate(weights)
    ]
    for load in own_loads:
        load.start()

    def pieces(w):
        src, buf = weights[w]
        n = buf.shape[2]
        return src, buf, n, n // 2

    def copy_of(w, kind, k, piece, to, device):
        return remote(piece, to, wsend.at[w, kind, k], wrecv.at[w, kind, k], device)

    def weight_begin(w):
        src, buf, n, m = pieces(w)
        copy_of(w, 0, 0, src, buf.at[1], mate).start()
        for k in range(n):
            copy_of(w, 1, k, src.at[z, k], buf.at[2, z, k], cross).start()
        half = pl.ds((1 - yl) * m, m)
        copy_of(w, 2, 0, src.at[zo, half], buf.at[2, zo, half], cross).start()

    def weight_quarter(w, k):
        _, buf, _, _ = pieces(w)
        piece = buf.at[2, z, k]
        copy_of(w, 1, k, piece, piece, cross).wait_recv()
        copy_of(w, 3, k, piece, piece, up).start()
        copy_of(w, 4, k, piece, piece, down).start()
        copy_of(w, 5, k, piece, buf.at[3, z, k], mate).start()

    def weight_half(w):
        _, buf, _, m = pieces(w)
        half = pl.ds(yl * m, m)
        piece = buf.at[2, zo, half]
        copy_of(w, 2, 0, piece, piece, cross).wait_recv()
        copy_of(w, 6, 0, piece, piece, beside).start()
        copy_of(w, 7, 0, piece, buf.at[3, zo, half], mate).start()

    def weight_rest(w):
        _, buf, n, m = pieces(w)
        for kind, zz in ((3, zd), (4, zu)):
            for k in range(n):
                piece = buf.at[2, zz, k]
                copy_of(w, kind, k, piece, piece, up).wait_recv()
            copy_of(w, 8, kind - 3, buf.at[2, zz], buf.at[3, zz], mate).start()
        half = pl.ds((1 - yl) * m, m)
        piece = buf.at[2, zo, half]
        copy_of(w, 6, 0, piece, piece, beside).wait_recv()
        copy_of(w, 8, 2, piece, buf.at[3, zo, half], mate).start()

    def weight_end(w):
        src, buf, n, m = pieces(w)
        own_loads[w].wait()
        copy_of(w, 0, 0, src, buf.at[1], mate).wait_recv()
        for k in range(n):
            piece = buf.at[3, z, k]
            copy_of(w, 5, k, piece, piece, mate).wait_recv()
        mine = buf.at[3, zo, pl.ds(yl * m, m)]
        copy_of(w, 7, 0, mine, mine, mate).wait_recv()
        for k, zz in ((0, zd), (1, zu)):
            piece = buf.at[3, zz]
            copy_of(w, 8, k, piece, piece, mate).wait_recv()
        other = buf.at[3, zo, pl.ds((1 - yl) * m, m)]
        copy_of(w, 8, 2, other, other, mate).wait_recv()

    def weight_sent(w):
        src, buf, n, m = pieces(w)
        piece, half, whole = buf.at[2, z, 0], buf.at[2, zo, pl.ds(yl * m, m)], buf.at[2, z]
        copy_of(w, 0, 0, src, buf.at[1], mate).wait_send()
        for kind, device in ((1, cross), (3, up), (4, down), (5, mate)):
            for k in range(n):
                copy_of(w, kind, k, piece, piece, device).wait_send()
        for kind, device in ((2, cross), (6, beside), (7, mate)):
            copy_of(w, kind, 0, half, half, device).wait_send()
        for k in range(2):
            copy_of(w, 8, k, whole, whole, mate).wait_send()
        copy_of(w, 8, 2, half, half, mate).wait_send()

    load_w.wait()
    m0 = smod[0:1, :]
    m0_high = m0.astype(BF).astype(F32)
    row = iota((16, d), 0)
    shift_rows = jnp.where(row == 0, m0_high, jnp.where(row == 1, m0 - m0_high, 0.0)).astype(BF)
    bias = jnp.sum(dot(shift_rows, wi[...]), axis=0, keepdims=True)

    def fold(i, _):
        rows = pl.ds(pl.multiple_of(i * 128, 128), 128)
        gain = jnp.broadcast_to(1.0 + smod[1:2, rows], (128, 128)).T
        for j in range(3):
            cols = slice(j * 128, (j + 1) * 128)
            wx[rows, cols] = (wi[rows, cols].astype(F32) * gain).astype(BF)
        wx[rows, 384:512] = jnp.ones((128, 128), BF)
        return 0

    lax.fori_loop(0, d // 128, fold, 0, unroll=4)
    colsum = dot(jnp.ones((16, d), BF), wx[:, 0:384])[0:1, :]

    def project(i, _):
        pltpu.make_async_copy(tok_in.at[i], tok.at[i], tok_sem.at[i]).wait()

        @pl.when(i == 2)
        def _():
            pl.semaphore_wait(barrier, len(partners))
            for w in range(3):
                weight_begin(w)

        t = tok[i]
        raw = dot(t, wx[...])
        base = t[:, 0:1].astype(F32)
        squares = jnp.zeros((320, 128), F32)
        for j in range(d // 128):
            e = t[:, j * 128:(j + 1) * 128].astype(F32) - base
            squares = squares + e * e
        mean = raw[:, 384:385] * (1.0 / d)
        spread = jnp.sum(squares, axis=1, keepdims=True) * (1.0 / d) - (mean - base) * (mean - base)
        scale = lax.rsqrt(spread + 1e-06)
        full = ((raw[:, 0:384] - mean * colsum) * scale + bias).astype(BF)
        rows = pl.ds(pl.multiple_of(i * 320, 320), 320)
        qb[rows, :] = full[:, 0:128]
        kb[rows, :] = full[:, 128:256]
        vx[rows, 0:128] = full[:, 256:384]
        vx[rows, 128:256] = jnp.ones((320, 128), BF)
        return 0

    lax.fori_loop(0, 4, project, 0)

    score_scale = 128 ** (-0.5) * LOG2E

    r256 = iota((256, 1), 0)
    spot = ((r256 >> 1) & 7) * 160 + ((r256 >> 4) & 3) * 40 + (r256 >> 6) * 10 + (r256 & 1)
    cells = iota((1, 1280), 1)

    def attend(b, _):
        queries = dot(one_hot(spot + 2 * b == cells), qb[...]).astype(BF)
        scores = dot_nt(queries, kb[...])
        top = jnp.max(scores, axis=1, keepdims=True)
        probs = jnp.exp2((scores - top) * score_scale).astype(BF)
        both = dot(probs, vx[...])
        att[b] = (both[:, 0:128] / both[:, 128:256]).astype(BF).reshape(4, 64, 128)
        for r in (2, 3, 1):
            remote(att.at[b, quarters[r]], cat.at[b, r], asend.at[b, r], arecv.at[b, r], quad[r]).start()

        @pl.when(b == 2)
        def _():
            weight_quarter(0, 0)
            weight_quarter(0, 1)

        return 0

    lax.fori_loop(0, nb, attend, 0)
    weight_half(0)

    first = h * 10
    start = jnp.minimum((first // 16) * 16, 128)
    skip = first - start
    r80 = iota((80, 1), 0)
    target = ((r80 >> 1) & 7) * 32 + (r80 >> 4) * 2 + (r80 & 1) + skip
    flat = tok.reshape(1280, d)
    windows = jnp.concatenate(
        [flat[pl.ds(pl.multiple_of(k * 160 + start, 16), 32), :] for k in range(8)], axis=0
    )
    own_rows[...] = dot(one_hot(target == iota((1, 256), 1)), windows).astype(BF)

    r128 = iota((128, 1), 0)
    c128 = iota((1, 128), 1)
    to_send = one_hot((r128 & 7) * 16 + (r128 >> 4) * 2 + ((r128 >> 3) & 1) == c128)
    from_recv = one_hot((r128 & 7) * 16 + ((r128 >> 3) & 1) * 8 + (r128 >> 4) == c128)
    lo, hi = pl.ds(0, hb), pl.ds(hb, hb)

    def ring_first(b, buf, rel, rec, ss, rs):
        remote(buf.at[b, xo, :, lo], rel.at[b, 0], ss.at[b, 0], rs.at[b, 0], right).start()
        remote(buf.at[b, xo, :, hi], rel.at[b, 1], ss.at[b, 1], rs.at[b, 1], left).start()
        remote(buf.at[b, xr, :, hi], rec.at[b, 0, 1], ss.at[b, 2], rs.at[b, 2], right).start()
        remote(buf.at[b, xl, :, lo], rec.at[b, 1, 0], ss.at[b, 3], rs.at[b, 3], left).start()

    def ring_second(b, buf, rel, rec, ss, rs):
        remote(rel.at[b, 0], rel.at[b, 0], ss.at[b, 0], rs.at[b, 0], right).wait_recv()
        rel[b, 0] = (rel[b, 0].astype(F32) + buf[b, xr, :, lo].astype(F32)).astype(BF)
        remote(rel.at[b, 0], rec.at[b, 0, 0], ss.at[b, 4], rs.at[b, 4], right).start()
        remote(rel.at[b, 1], rel.at[b, 1], ss.at[b, 1], rs.at[b, 1], left).wait_recv()
        rel[b, 1] = (rel[b, 1].astype(F32) + buf[b, xl, :, hi].astype(F32)).astype(BF)
        remote(rel.at[b, 1], rec.at[b, 1, 1], ss.at[b, 5], rs.at[b, 5], left).start()

    def ring_last(b, buf, rec, ss, rs):
        for k, side, half in ((2, 0, 1), (3, 1, 0), (4, 0, 0), (5, 1, 1)):
            piece = rec.at[b, side, half]
            remote(piece, piece, ss.at[b, k], rs.at[b, k], right).wait_recv()
        own = buf[b, x].astype(F32)
        halves = [
            own[:, k * hb:(k + 1) * hb] + rec[b, 0, k].astype(F32) + rec[b, 1, k].astype(F32)
            for k in range(2)
        ]
        return jnp.concatenate(halves, axis=1)

    def ring_sent(b, rel, ss, rs):
        for k in range(6):
            remote(rel.at[b, 0], rel.at[b, 0], ss.at[b, k], rs.at[b, k], right).wait_send()

    def sum_begin(b):
        for r in (1, 2, 3):
            remote(cat.at[b, r], cat.at[b, r], asend.at[b, r], arecv.at[b, r], quad[r]).wait_recv()
        lhs = jnp.concatenate([att[b, q], cat[b, 1], cat[b, 2], cat[b, 3]], axis=1)
        part[b] = dot(lhs, wo[...].reshape(512, d)).astype(BF).reshape(4, 16, d)
        ring_first(b, part, relay, got, rsend, rrecv)

    def swap_send(b):
        total = ring_last(b, part, got, rsend, rrecv)
        rows = own_rows[pl.ds(pl.multiple_of(b * 16, 16), 16), :]
        middle = (rows.astype(F32) + smod[2:3, :] * total).astype(BF)
        stacked = jnp.concatenate([middle[:, k * eighth:(k + 1) * eighth] for k in range(8)], axis=0)
        shuf[b] = dot(to_send, stacked).astype(BF).reshape(8, 16, eighth)
        for j in (4, 1, 7, 5, 3, 2, 6):
            to = (s + j) % 8
            remote(shuf.at[b, to], shufr.at[b, s], ssend.at[b, j], srecv.at[b, j], (to, h)).start()
        shufr[b, s] = shuf[b, s]

    def gather_send(b):
        for j in range(1, 8):
            piece = shufr.at[b, (s + 8 - j) % 8]
            remote(piece, piece, ssend.at[b, j], srecv.at[b, j], right).wait_recv()
        rows = dot(from_recv, shufr[b].reshape(128, eighth)).astype(BF)
        gath[b, x] = jnp.concatenate([rows[k * 16:(k + 1) * 16, :] for k in range(8)], axis=1)
        mine = gath.at[b, x]
        remote(mine, mine, gsend.at[b, 0], grecv.at[b, 0], right).start()
        remote(mine, mine, gsend.at[b, 1], grecv.at[b, 1], left).start()

    def gather_relay(b):
        from_left, from_right = gath.at[b, xl], gath.at[b, xr]
        remote(from_left, from_left, gsend.at[b, 0], grecv.at[b, 0], right).wait_recv()
        piece = gath.at[b, xl, :, lo]
        remote(piece, piece, gsend.at[b, 2], grecv.at[b, 2], right).start()
        remote(from_right, from_right, gsend.at[b, 1], grecv.at[b, 1], left).wait_recv()
        piece = gath.at[b, xr, :, hi]
        remote(piece, piece, gsend.at[b, 3], grecv.at[b, 3], left).start()

    same = (iota((64, 64), 0) >> 3) == (iota((64, 64), 1) >> 3)

    def temporal(b):
        far = gath.at[b, xo]
        remote(far.at[:, lo], far.at[:, lo], gsend.at[b, 2], grecv.at[b, 2], right).wait_recv()
        remote(far.at[:, hi], far.at[:, hi], gsend.at[b, 3], grecv.at[b, 3], left).wait_recv()
        rows = gath[b].reshape(64, d).astype(F32)
        center = rows - jnp.sum(rows, axis=1, keepdims=True) * (1.0 / d)
        spread = jnp.sum(center * center, axis=1, keepdims=True) * (1.0 / d)
        scale = lax.rsqrt(spread + 1e-06)
        normed = (center * scale * (1.0 + tmod[1:2, :]) + tmod[0:1, :]).astype(BF)

        @pl.when(b == 0)
        def _():
            weight_rest(1)
            weight_end(1)

        attended = []
        for j in range(4):
            joined = dot(normed, wt[j].reshape(d, 384)).astype(BF)
            scores = dot_nt(joined[:, 0:128], joined[:, 128:256])
            scores = jnp.where(same, scores, -1e30)
            top = jnp.max(scores, axis=1, keepdims=True)
            probs = jnp.exp2((scores - top) * score_scale)
            probs = (probs / jnp.sum(probs, axis=1, keepdims=True)).astype(BF)
            attended.append(dot(probs, joined[:, 256:384]).astype(BF))

        @pl.when(b == 0)
        def _():
            weight_rest(2)
            weight_end(2)

        lhs = jnp.concatenate(attended, axis=1)
        part2[b] = dot(lhs, wto[...].reshape(512, d)).astype(BF).reshape(4, 16, d)
        ring_first(b, part2, relay2, got2, rsend2, rrecv2)

    def finish(b):
        total = ring_last(b, part2, got2, rsend2, rrecv2)
        res[b] = (gath[b, x].astype(F32) + tmod[2:3, :] * total).astype(BF)
        rows = pl.ds(pl.multiple_of(b * 16, 16), 16)
        pltpu.make_async_copy(res.at[b], out.at[rows, :], out_sem.at[b]).start()

    weight_rest(0)
    weight_end(0)

    stages = (
        sum_begin,
        lambda b: ring_second(b, part, relay, got, rsend, rrecv),
        swap_send,
        gather_send,
        gather_relay,
        temporal,
        lambda b: ring_second(b, part2, relay2, got2, rsend2, rrecv2),
        finish,
    )

    def tick(t, _):
        for k, stage in enumerate(stages):
            @pl.when((t >= k) & (t < k + nb))
            def _(stage=stage, k=k):
                stage(t - k)

        for when, move in TICKS:
            @pl.when(t == when)
            def _(move=move):
                if len(move) == 1:
                    weight_half(*move)
                else:
                    weight_quarter(*move)

        return 0

    lax.fori_loop(0, nb + len(stages) - 1, tick, 0)

    for b in range(nb):
        pltpu.make_async_copy(res.at[b], out.at[pl.ds(b * 16, 16), :], out_sem.at[b]).wait()

    def sent(b, _):
        for r in (1, 2, 3):
            remote(cat.at[b, r], cat.at[b, r], asend.at[b, r], arecv.at[b, r], quad[r]).wait_send()
        ring_sent(b, relay, rsend, rrecv)
        ring_sent(b, relay2, rsend2, rrecv2)
        for j in range(1, 8):
            piece = shuf.at[b, 0]
            remote(piece, piece, ssend.at[b, j], srecv.at[b, j], right).wait_send()
        for k in range(4):
            piece = gath.at[b, x] if k < 2 else gath.at[b, x, :, lo]
            remote(piece, piece, gsend.at[b, k], grecv.at[b, k], right).wait_send()
        return 0

    lax.fori_loop(0, nb, sent, 0)
    for w in range(3):
        weight_sent(w)


def shards(
    tokens, spatial_modulation, spatial_weights_in, spatial_weights_out,
    temporal_modulation, temporal_weights_in, temporal_weights_out,
):
    d = tokens.shape[-1]
    nb = BLOCKS
    hb = d // 2
    dma = pltpu.SemaphoreType.DMA
    any_space = pl.BlockSpec(memory_space=pl.ANY)
    vmem = pl.BlockSpec(memory_space=pltpu.VMEM)
    out_weights = pltpu.VMEM((4, 4, 2, 16, d), BF)
    ring = [
        pltpu.VMEM((nb, 4, 16, d), BF),
        pltpu.VMEM((nb, 2, 16, hb), BF),
        pltpu.VMEM((nb, 2, 2, 16, hb), BF),
    ]
    result = pl.pallas_call(
        kernel,
        out_shape=jax.ShapeDtypeStruct((80, d), BF),
        in_specs=[any_space, vmem, any_space, any_space, vmem, any_space, any_space],
        out_specs=any_space,
        scratch_shapes=[
            pltpu.VMEM((4, 320, d), BF),
            pltpu.VMEM((d, 384), BF),
            pltpu.VMEM((d, 512), BF),
            pltpu.VMEM((1280, 128), BF),
            pltpu.VMEM((1280, 128), BF),
            pltpu.VMEM((1280, 256), BF),
            pltpu.VMEM((nb, 4, 64, 128), BF),
            pltpu.VMEM((nb, 4, 64, 128), BF),
            pltpu.VMEM((80, d), BF),
            out_weights,
            pltpu.VMEM((4, 4, 4, d // 16, 384), BF),
            out_weights,
            *ring,
            pltpu.VMEM((nb, 8, 16, d // 8), BF),
            pltpu.VMEM((nb, 8, 16, d // 8), BF),
            pltpu.VMEM((nb, 4, 16, d), BF),
            *ring,
            pltpu.VMEM((nb, 16, d), BF),
            dma((3,)), dma((4,)), dma((nb,)), dma(()),
            dma((3, 9, 4)), dma((3, 9, 4)),
            dma((nb, 4)), dma((nb, 4)),
            dma((nb, 6)), dma((nb, 6)),
            dma((nb, 8)), dma((nb, 8)),
            dma((nb, 4)), dma((nb, 4)),
            dma((nb, 6)), dma((nb, 6)),
        ],
        compiler_params=pltpu.CompilerParams(
            collective_id=0, has_side_effects=True, vmem_limit_bytes=60 * 1024 * 1024
        ),
        cost_estimate=pl.CostEstimate(
            flops=9_000_000_000, bytes_accessed=16_000_000, transcendentals=2_000_000
        ),
    )(
        tokens.reshape(4, 320, d),
        spatial_modulation,
        jnp.transpose(spatial_weights_in, (1, 0, 2)).reshape(d, 384),
        spatial_weights_out.reshape(4, 2, 16, d),
        temporal_modulation,
        jnp.transpose(temporal_weights_in, (1, 0, 2)).reshape(4, 4, d // 16, 384),
        temporal_weights_out.reshape(4, 2, 16, d),
    )
    return jnp.transpose(result.reshape(10, 8, d), (1, 0, 2))


def solution(mesh):
    placed = (
        P("seq", None, None),
        P(),
        P(None, "head", None),
        P("head", None, None),
        P(),
        P(None, "head", None),
        P("head", None, None),
    )
    return jax.shard_map(
        shards,
        mesh=mesh,
        in_specs=placed,
        out_specs=P(None, ("seq", "head"), None),
        check_vma=False,
    )
```

time: 121 us -> 110 us (0.909); the launches traced: 120 us -> 108 us
  Pallas kernels: 119 us -> 106 us
    pallas_call x1, Pallas kernels: 119 us -> 106 us  [shards(): pl.pallas_call(kernel, out_shape=jax.ShapeDtypeStruct((80, d), BF), in_sp...]
where the time goes in v2:
time: 110 us; the launch traced here: 108 us
  Pallas kernels  106 us (96%)
  local copies, waits for them, and re-layouts  1.84 us (2%)
    pallas_call x1, Pallas kernels, shards(): pl.pallas_call(kernel, out_shape=jax.ShapeDtypeStruct((80, d), BF), in_sp...  106 us

profile of v2, /device:TPU:0, one launch (start us, length us, event | category | flops | bytes accessed | tf_op | source)
XLA Modules:
  0.0 107.9 jit_solution(6148716976908404387)
XLA Ops:
  0.0 106.0 %shard_map.73 = bf16[80,3072]{1,0:T(8,128)(2,1)} custom-call(bf16[4,320,3072]{2,1,0:T(8,128)(2,1)} %bitcast.9, f32[3,3072]{1,0:T(4,128)} %smod.1, bf16[3072,384]{1,0:T(8,128)(2,1)} %bitcast.10, bf16[4,2,16,3072]{3,2,1,0:T(8,128)(2,1)} %bitcast.12, f32[3,3072]{1,0:T(4,128)} %tmod.1, bf16[4,4,192,384]{3,2,1,0:T(8,128)(2,1)} %bitcast.11, ...), custom_call_target="tpu_custom_call" | custom-call | flops 8999999488 | bytes 16000000 | tf_op jit(solution)/shard_map/pallas_call | solution.py:428
  106.0 1.8 %copy.9 = bf16[8,10,3072]{2,0,1:T(8,128)(2,1)} copy(bf16[8,10,3072]{2,0,1:T(8,128)(2,1)} %bitcast.8) | data formatting | bytes 983040

commit v3 on v2

--- a/solution.py
+++ b/solution.py
@@ -12,9 +12,32 @@
 MESH = pl.DeviceIdType.MESH
 BLOCKS = 5
 LOG2E = 1.4426950408889634
-TICKS = (
-    (0, (1, 0)), (0, (1, 1)), (1, (1, 2)), (1, (1, 3)), (2, (1,)), (3, (2, 0)), (3, (2, 1)), (4, (2,)),
+TABLE = (
+    ("attend", (0, 0), (1, 1), (2, 2), (4, 3), (5, 4)),
+    ("rest", 2, 0),
+    ("sum_begin", (2, 0), (3, 1), (4, 2), (7, 3), (8, 4)),
+    ("sum_second", (5, 0), (6, 1), (7, 2), (9, 3), (10, 4)),
+    ("swap_send", (7, 0), (8, 1), (10, 2), (11, 3), (12, 4)),
+    ("gather_send", (9, 0), (10, 1), (11, 2), (12, 3), (14, 4)),
+    ("gather_relay", (11, 0), (12, 1), (13, 2), (14, 3), (15, 4)),
+    ("rest", 12, 1),
+    ("rest", 14, 2),
+    ("temporal", 14, 0, 2),
+    ("temporal", 15, 2, 4),
+    ("temporal", 17, 4, 5),
+    ("back_second", (15, 0), (16, 1), (17, 2), (18, 3), (19, 4)),
+    ("finish", (17, 0), (18, 1), (19, 2), (20, 3), (21, 4)),
+    ("quarter", 0, 1, 0),
+    ("quarter", 4, 1, 1),
+    ("quarter", 5, 1, 2),
+    ("quarter", 8, 1, 3),
+    ("quarter", 11, 2, 0),
+    ("quarter", 12, 2, 1),
+    ("half", 4, 1),
+    ("half", 11, 2),
 )
+COUNT = 22
+CROSS = ((0, 0), (0, 1), (0, -1), (1, 0), (1, 1), (1, -1), (1, 2), (1, 3), (2, 0), (2, 1), (2, -1))
 
 
 def dot(a, b):
@@ -80,82 +103,95 @@
         pltpu.make_async_copy(tok_in.at[i], tok.at[i], tok_sem.at[i]).start()
     weights = ((wo_in, wo), (wt_in, wt), (wto_in, wto))
     own_loads = [
-        pltpu.make_async_copy(src, dst.at[0], local_sem.at[i]) for i, (src, dst) in enumerate(weights)
+        pltpu.make_async_copy(wo_in, wo.at[0], local_sem.at[0]),
+        pltpu.make_async_copy(wt_in, wt.at[:, :, :, pl.ds(0, 384)], local_sem.at[1]),
+        pltpu.make_async_copy(wto_in, wto.at[0], local_sem.at[2]),
     ]
     for load in own_loads:
         load.start()
 
-    def pieces(w):
-        src, buf = weights[w]
-        n = buf.shape[2]
-        return src, buf, n, n // 2
+    counts = (2, 4, 2)
+
+    def at(w, slot, *where):
+        buf = weights[w][1]
+        if w == 1:
+            where = where + (slice(None),) * (3 - len(where))
+            return buf.at[where + (pl.ds(slot * 384, 384),)]
+        return buf.at[(slot,) + where]
 
     def copy_of(w, kind, k, piece, to, device):
         return remote(piece, to, wsend.at[w, kind, k], wrecv.at[w, kind, k], device)
 
-    def weight_begin(w):
-        src, buf, n, m = pieces(w)
-        copy_of(w, 0, 0, src, buf.at[1], mate).start()
-        for k in range(n):
-            copy_of(w, 1, k, src.at[z, k], buf.at[2, z, k], cross).start()
-        half = pl.ds((1 - yl) * m, m)
-        copy_of(w, 2, 0, src.at[zo, half], buf.at[2, zo, half], cross).start()
+    def halves(w):
+        m = counts[w] // 2
+        return pl.ds(yl * m, m), pl.ds((1 - yl) * m, m)
+
+    def weight_near(w):
+        copy_of(w, 0, 0, weights[w][0], at(w, 1), mate).start()
+
+    def weight_cross(w, k):
+        copy_of(w, 1, k, weights[w][0].at[z, k], at(w, 2, z, k), cross).start()
+
+    def weight_cross_half(w):
+        theirs = halves(w)[1]
+        copy_of(w, 2, 0, weights[w][0].at[zo, theirs], at(w, 2, zo, theirs), cross).start()
 
     def weight_quarter(w, k):
-        _, buf, _, _ = pieces(w)
-        piece = buf.at[2, z, k]
+        piece = at(w, 2, z, k)
         copy_of(w, 1, k, piece, piece, cross).wait_recv()
         copy_of(w, 3, k, piece, piece, up).start()
         copy_of(w, 4, k, piece, piece, down).start()
-        copy_of(w, 5, k, piece, buf.at[3, z, k], mate).start()
+        copy_of(w, 5, k, piece, at(w, 3, z, k), mate).start()
 
     def weight_half(w):
-        _, buf, _, m = pieces(w)
-        half = pl.ds(yl * m, m)
-        piece = buf.at[2, zo, half]
+        mine = halves(w)[0]
+        piece = at(w, 2, zo, mine)
         copy_of(w, 2, 0, piece, piece, cross).wait_recv()
         copy_of(w, 6, 0, piece, piece, beside).start()
-        copy_of(w, 7, 0, piece, buf.at[3, zo, half], mate).start()
+        copy_of(w, 7, 0, piece, at(w, 3, zo, mine), mate).start()
 
     def weight_rest(w):
-        _, buf, n, m = pieces(w)
         for kind, zz in ((3, zd), (4, zu)):
-            for k in range(n):
-                piece = buf.at[2, zz, k]
+            for k in range(counts[w]):
+                piece = at(w, 2, zz, k)
                 copy_of(w, kind, k, piece, piece, up).wait_recv()
-            copy_of(w, 8, kind - 3, buf.at[2, zz], buf.at[3, zz], mate).start()
-        half = pl.ds((1 - yl) * m, m)
-        piece = buf.at[2, zo, half]
+            copy_of(w, 8, kind - 3, at(w, 2, zz), at(w, 3, zz), mate).start()
+        theirs = halves(w)[1]
+        piece = at(w, 2, zo, theirs)
         copy_of(w, 6, 0, piece, piece, beside).wait_recv()
-        copy_of(w, 8, 2, piece, buf.at[3, zo, half], mate).start()
+        copy_of(w, 8, 2, piece, at(w, 3, zo, theirs), mate).start()
 
     def weight_end(w):
-        src, buf, n, m = pieces(w)
+        mine, theirs = halves(w)
         own_loads[w].wait()
-        copy_of(w, 0, 0, src, buf.at[1], mate).wait_recv()
-        for k in range(n):
-            piece = buf.at[3, z, k]
-            copy_of(w, 5, k, piece, piece, mate).wait_recv()
-        mine = buf.at[3, zo, pl.ds(yl * m, m)]
-        copy_of(w, 7, 0, mine, mine, mate).wait_recv()
+        copy_of(w, 0, 0, weights[w][0], at(w, 1), mate).wait_recv()
+        for k in range(counts[w]):
+            copy_of(w, 5, k, at(w, 3, z, k), at(w, 3, z, k), mate).wait_recv()
+        copy_of(w, 7, 0, at(w, 3, zo, mine), at(w, 3, zo, mine), mate).wait_recv()
         for k, zz in ((0, zd), (1, zu)):
-            piece = buf.at[3, zz]
-            copy_of(w, 8, k, piece, piece, mate).wait_recv()
-        other = buf.at[3, zo, pl.ds((1 - yl) * m, m)]
-        copy_of(w, 8, 2, other, other, mate).wait_recv()
+            copy_of(w, 8, k, at(w, 3, zz), at(w, 3, zz), mate).wait_recv()
+        copy_of(w, 8, 2, at(w, 3, zo, theirs), at(w, 3, zo, theirs), mate).wait_recv()
 
     def weight_sent(w):
-        src, buf, n, m = pieces(w)
-        piece, half, whole = buf.at[2, z, 0], buf.at[2, zo, pl.ds(yl * m, m)], buf.at[2, z]
-        copy_of(w, 0, 0, src, buf.at[1], mate).wait_send()
+        piece, half, whole = at(w, 2, z, 0), at(w, 2, zo, halves(w)[0]), at(w, 2, z)
+        copy_of(w, 0, 0, weights[w][0], at(w, 1), mate).wait_send()
         for kind, device in ((1, cross), (3, up), (4, down), (5, mate)):
-            for k in range(n):
+            for k in range(counts[w]):
                 copy_of(w, kind, k, piece, piece, device).wait_send()
         for kind, device in ((2, cross), (6, beside), (7, mate)):
             copy_of(w, kind, 0, half, half, device).wait_send()
         for k in range(2):
             copy_of(w, 8, k, whole, whole, mate).wait_send()
         copy_of(w, 8, 2, half, half, mate).wait_send()
+
+    pl.semaphore_wait(barrier, len(partners))
+    for w, k in CROSS:
+        if k < 0:
+            weight_cross_half(w)
+        else:
+            weight_cross(w, k)
+    for w in range(3):
+        weight_near(w)
 
     load_w.wait()
     m0 = smod[0:1, :]
@@ -179,11 +215,11 @@
     def project(i, _):
         pltpu.make_async_copy(tok_in.at[i], tok.at[i], tok_sem.at[i]).wait()
 
-        @pl.when(i == 2)
+        @pl.when(i == 3)
         def _():
-            pl.semaphore_wait(barrier, len(partners))
-            for w in range(3):
-                weight_begin(w)
+            weight_quarter(0, 0)
+            weight_quarter(0, 1)
+            weight_half(0)
 
         t = tok[i]
         raw = dot(t, wx[...])
@@ -211,7 +247,7 @@
     spot = ((r256 >> 1) & 7) * 160 + ((r256 >> 4) & 3) * 40 + (r256 >> 6) * 10 + (r256 & 1)
     cells = iota((1, 1280), 1)
 
-    def attend(b, _):
+    def attend(b):
         queries = dot(one_hot(spot + 2 * b == cells), qb[...]).astype(BF)
         scores = dot_nt(queries, kb[...])
         top = jnp.max(scores, axis=1, keepdims=True)
@@ -221,15 +257,6 @@
         for r in (2, 3, 1):
             remote(att.at[b, quarters[r]], cat.at[b, r], asend.at[b, r], arecv.at[b, r], quad[r]).start()
 
-        @pl.when(b == 2)
-        def _():
-            weight_quarter(0, 0)
-            weight_quarter(0, 1)
-
-        return 0
-
-    lax.fori_loop(0, nb, attend, 0)
-    weight_half(0)
 
     first = h * 10
     start = jnp.minimum((first // 16) * 16, 128)
@@ -278,6 +305,10 @@
             remote(rel.at[b, 0], rel.at[b, 0], ss.at[b, k], rs.at[b, k], right).wait_send()
 
     def sum_begin(b):
+        @pl.when(b == 0)
+        def _():
+            weight_end(0)
+
         for r in (1, 2, 3):
             remote(cat.at[b, r], cat.at[b, r], asend.at[b, r], arecv.at[b, r], quad[r]).wait_recv()
         lhs = jnp.concatenate([att[b, q], cat[b, 1], cat[b, 2], cat[b, 3]], axis=1)
@@ -314,41 +345,38 @@
         piece = gath.at[b, xr, :, hi]
         remote(piece, piece, gsend.at[b, 3], grecv.at[b, 3], left).start()
 
-    same = (iota((64, 64), 0) >> 3) == (iota((64, 64), 1) >> 3)
-
-    def temporal(b):
-        far = gath.at[b, xo]
-        remote(far.at[:, lo], far.at[:, lo], gsend.at[b, 2], grecv.at[b, 2], right).wait_recv()
-        remote(far.at[:, hi], far.at[:, hi], gsend.at[b, 3], grecv.at[b, 3], left).wait_recv()
-        rows = gath[b].reshape(64, d).astype(F32)
+    def temporal(lead, last):
+        n = (last - lead) * 64
+        for b in range(lead, last):
+            far = gath.at[b, xo]
+            remote(far.at[:, lo], far.at[:, lo], gsend.at[b, 2], grecv.at[b, 2], right).wait_recv()
+            remote(far.at[:, hi], far.at[:, hi], gsend.at[b, 3], grecv.at[b, 3], left).wait_recv()
+        rows = gath[lead:last].reshape(n, d).astype(F32)
         center = rows - jnp.sum(rows, axis=1, keepdims=True) * (1.0 / d)
         spread = jnp.sum(center * center, axis=1, keepdims=True) * (1.0 / d)
         scale = lax.rsqrt(spread + 1e-06)
         normed = (center * scale * (1.0 + tmod[1:2, :]) + tmod[0:1, :]).astype(BF)
-
-        @pl.when(b == 0)
-        def _():
-            weight_rest(1)
+        if lead == 0:
             weight_end(1)
-
+        joined = dot(normed, wt[...].reshape(d, 1536)).astype(BF)
+        same = (iota((n, n), 0) >> 3) == (iota((n, n), 1) >> 3)
         attended = []
         for j in range(4):
-            joined = dot(normed, wt[j].reshape(d, 384)).astype(BF)
-            scores = dot_nt(joined[:, 0:128], joined[:, 128:256])
-            scores = jnp.where(same, scores, -1e30)
+            mine = joined[:, j * 384:(j + 1) * 384]
+            scores = jnp.where(same, dot_nt(mine[:, 0:128], mine[:, 128:256]), -1e30)
             top = jnp.max(scores, axis=1, keepdims=True)
             probs = jnp.exp2((scores - top) * score_scale)
             probs = (probs / jnp.sum(probs, axis=1, keepdims=True)).astype(BF)
-            attended.append(dot(probs, joined[:, 256:384]).astype(BF))
-
-        @pl.when(b == 0)
-        def _():
-            weight_rest(2)
+            attended.append(dot(probs, mine[:, 256:384]).astype(BF))
+        if lead == 0:
             weight_end(2)
-
         lhs = jnp.concatenate(attended, axis=1)
-        part2[b] = dot(lhs, wto[...].reshape(512, d)).astype(BF).reshape(4, 16, d)
-        ring_first(b, part2, relay2, got2, rsend2, rrecv2)
+        part2[lead:last] = dot(lhs, wto[...].reshape(512, d)).astype(BF).reshape(last - lead, 4, 16, d)
+        for b in range(lead, last):
+            ring_first(b, part2, relay2, got2, rsend2, rrecv2)
+
+    def back_second(b):
+        ring_second(b, part2, relay2, got2, rsend2, rrecv2)
 
     def finish(b):
         total = ring_last(b, part2, got2, rsend2, rrecv2)
@@ -356,37 +384,34 @@
         rows = pl.ds(pl.multiple_of(b * 16, 16), 16)
         pltpu.make_async_copy(res.at[b], out.at[rows, :], out_sem.at[b]).start()
 
-    weight_rest(0)
-    weight_end(0)
-
-    stages = (
-        sum_begin,
-        lambda b: ring_second(b, part, relay, got, rsend, rrecv),
-        swap_send,
-        gather_send,
-        gather_relay,
-        temporal,
-        lambda b: ring_second(b, part2, relay2, got2, rsend2, rrecv2),
-        finish,
-    )
+    def sum_second(b):
+        ring_second(b, part, relay, got, rsend, rrecv)
+
+    blocks = {
+        "attend": attend, "sum_begin": sum_begin, "sum_second": sum_second, "swap_send": swap_send,
+        "gather_send": gather_send, "gather_relay": gather_relay, "back_second": back_second, "finish": finish,
+    }
+    moves = {"temporal": temporal, "quarter": weight_quarter, "half": weight_half, "rest": weight_rest}
 
     def tick(t, _):
-        for k, stage in enumerate(stages):
-            @pl.when((t >= k) & (t < k + nb))
-            def _(stage=stage, k=k):
-                stage(t - k)
-
-        for when, move in TICKS:
-            @pl.when(t == when)
-            def _(move=move):
-                if len(move) == 1:
-                    weight_half(*move)
-                else:
-                    weight_quarter(*move)
+        for name, *what in TABLE:
+            if name in blocks:
+                hit, b = t < 0, 0
+                for when, block in what:
+                    hit = hit | (t == when)
+                    b = b + jnp.where(t == when, block, 0)
+
+                @pl.when(hit)
+                def _(name=name, b=b):
+                    blocks[name](b)
+            else:
+                @pl.when(t == what[0])
+                def _(name=name, what=what):
+                    moves[name](*what[1:])
 
         return 0
 
-    lax.fori_loop(0, nb + len(stages) - 1, tick, 0)
+    lax.fori_loop(0, COUNT, tick, 0)
 
     for b in range(nb):
         pltpu.make_async_copy(res.at[b], out.at[pl.ds(b * 16, 16), :], out_sem.at[b]).wait()
@@ -441,7 +466,7 @@
             pltpu.VMEM((nb, 4, 64, 128), BF),
             pltpu.VMEM((80, d), BF),
             out_weights,
-            pltpu.VMEM((4, 4, 4, d // 16, 384), BF),
+            pltpu.VMEM((4, 4, d // 16, 1536), BF),
             out_weights,
             *ring,
             pltpu.VMEM((nb, 8, 16, d // 8), BF),

time: 110 us -> 89 us (0.81); the launches traced: 108 us -> 88.8 us
  Pallas kernels: 106 us -> 87 us
    pallas_call x1, Pallas kernels: 106 us -> 87 us  [shards(): pl.pallas_call(kernel, out_shape=jax.ShapeDtypeStruct((80, d), BF), in_sp...]
where the time goes in v3:
time: 89 us; the launch traced here: 88.8 us
  Pallas kernels  87 us (98%)
  local copies, waits for them, and re-layouts  1.84 us (2%)
    pallas_call x1, Pallas kernels, shards(): pl.pallas_call(kernel, out_shape=jax.ShapeDtypeStruct((80, d), BF), in_sp...  87 us
    unnamed x1, local copies, waits for them, and re-layouts  1.84 us

profile of v3, /device:TPU:0, one launch (start us, length us, event | category | flops | bytes accessed | tf_op | source)
XLA Modules:
  0.0 88.8 jit_solution(10605243072100135792)
XLA Ops:
  0.0 87.0 %shard_map.73 = bf16[80,3072]{1,0:T(8,128)(2,1)} custom-call(bf16[4,320,3072]{2,1,0:T(8,128)(2,1)} %bitcast.9, f32[3,3072]{1,0:T(4,128)} %smod.1, bf16[3072,384]{1,0:T(8,128)(2,1)} %bitcast.10, bf16[4,2,16,3072]{3,2,1,0:T(8,128)(2,1)} %bitcast.12, f32[3,3072]{1,0:T(4,128)} %tmod.1, bf16[4,4,192,384]{3,2,1,0:T(8,128)(2,1)} %bitcast.11, ...), custom_call_target="tpu_custom_call" | custom-call | flops 8999999488 | bytes 16000000 | tf_op jit(solution)/shard_map/pallas_call | solution.py:453
  87.0 1.8 %copy.9 = bf16[8,10,3072]{2,0,1:T(8,128)(2,1)} copy(bf16[8,10,3072]{2,0,1:T(8,128)(2,1)} %bitcast.8) | data formatting | bytes 983040

commit v4 on v3

--- a/solution.py
+++ b/solution.py
@@ -13,31 +13,31 @@
 BLOCKS = 5
 LOG2E = 1.4426950408889634
 TABLE = (
-    ("attend", (0, 0), (1, 1), (2, 2), (4, 3), (5, 4)),
-    ("rest", 2, 0),
-    ("sum_begin", (2, 0), (3, 1), (4, 2), (7, 3), (8, 4)),
-    ("sum_second", (5, 0), (6, 1), (7, 2), (9, 3), (10, 4)),
-    ("swap_send", (7, 0), (8, 1), (10, 2), (11, 3), (12, 4)),
+    ("attend", (0, 0), (1, 1), (2, 2), (5, 3), (6, 4)),
+    ("rest", 1, 0),
+    ("sum_begin", (3, 0), (4, 1), (5, 2), (7, 3), (8, 4)),
+    ("sum_second", (5, 0), (6, 1), (7, 2), (8, 3), (10, 4)),
+    ("swap_send", (7, 0), (8, 1), (9, 2), (10, 3), (12, 4)),
     ("gather_send", (9, 0), (10, 1), (11, 2), (12, 3), (14, 4)),
     ("gather_relay", (11, 0), (12, 1), (13, 2), (14, 3), (15, 4)),
-    ("rest", 12, 1),
-    ("rest", 14, 2),
+    ("rest", 13, 1),
+    ("rest", 13, 2),
     ("temporal", 14, 0, 2),
     ("temporal", 15, 2, 4),
     ("temporal", 17, 4, 5),
     ("back_second", (15, 0), (16, 1), (17, 2), (18, 3), (19, 4)),
     ("finish", (17, 0), (18, 1), (19, 2), (20, 3), (21, 4)),
     ("quarter", 0, 1, 0),
-    ("quarter", 4, 1, 1),
-    ("quarter", 5, 1, 2),
-    ("quarter", 8, 1, 3),
-    ("quarter", 11, 2, 0),
-    ("quarter", 12, 2, 1),
-    ("half", 4, 1),
-    ("half", 11, 2),
+    ("quarter", 2, 1, 1),
+    ("quarter", 4, 1, 2),
+    ("quarter", 5, 1, 3),
+    ("quarter", 6, 2, 0),
+    ("quarter", 7, 2, 1),
+    ("relay", 9, 1, 0),
+    ("relay", 10, 1, 1),
+    ("relay", 12, 2, 0),
 )
 COUNT = 22
-CROSS = ((0, 0), (0, 1), (0, -1), (1, 0), (1, 1), (1, -1), (1, 2), (1, 3), (2, 0), (2, 1), (2, -1))
 
 
 def dot(a, b):
@@ -66,7 +66,7 @@
 def kernel(
     tok_in, smod, win_in, wo_in, tmod, wt_in, wto_in,
     out,
-    tok, wi, wx, qb, kb, vx, att, cat, own_rows, wo, wt, wto,
+    tok, shift, wi, wx, qb, kb, vx, att, cat, own_rows, wo, wt, wto,
     part, relay, got, shuf, shufr, gath, part2, relay2, got2, res,
     local_sem, tok_sem, out_sem, win_sem, wsend, wrecv, asend, arecv,
     rsend, rrecv, ssend, srecv, gsend, grecv, rsend2, rrecv2,
@@ -100,7 +100,7 @@
     load_w = pltpu.make_async_copy(win_in, wi, win_sem)
     load_w.start()
     for i in range(4):
-        pltpu.make_async_copy(tok_in.at[i], tok.at[i], tok_sem.at[i]).start()
+        pltpu.make_async_copy(tok_in.at[i], tok.at[i, pl.ds(0, 320)], tok_sem.at[i]).start()
     weights = ((wo_in, wo), (wt_in, wt), (wto_in, wto))
     own_loads = [
         pltpu.make_async_copy(wo_in, wo.at[0], local_sem.at[0]),
@@ -122,74 +122,85 @@
     def copy_of(w, kind, k, piece, to, device):
         return remote(piece, to, wsend.at[w, kind, k], wrecv.at[w, kind, k], device)
 
-    def halves(w):
-        m = counts[w] // 2
-        return pl.ds(yl * m, m), pl.ds((1 - yl) * m, m)
+    def first_quarter(step):
+        return (z + 2 * yl + step) % 4
 
     def weight_near(w):
         copy_of(w, 0, 0, weights[w][0], at(w, 1), mate).start()
 
-    def weight_cross(w, k):
-        copy_of(w, 1, k, weights[w][0].at[z, k], at(w, 2, z, k), cross).start()
-
-    def weight_cross_half(w):
-        theirs = halves(w)[1]
-        copy_of(w, 2, 0, weights[w][0].at[zo, theirs], at(w, 2, zo, theirs), cross).start()
+    def weight_cross(w):
+        for k in range(counts[w]):
+            quarter = z if w else first_quarter(2)
+            copy_of(w, 1, k, weights[w][0].at[quarter, k], at(w, 2, quarter, k), cross).start()
 
     def weight_quarter(w, k):
-        piece = at(w, 2, z, k)
+        quarter = z if w else first_quarter(0)
+        piece = at(w, 2, quarter, k)
         copy_of(w, 1, k, piece, piece, cross).wait_recv()
         copy_of(w, 3, k, piece, piece, up).start()
         copy_of(w, 4, k, piece, piece, down).start()
-        copy_of(w, 5, k, piece, at(w, 3, z, k), mate).start()
-
-    def weight_half(w):
-        mine = halves(w)[0]
-        piece = at(w, 2, zo, mine)
-        copy_of(w, 2, 0, piece, piece, cross).wait_recv()
-        copy_of(w, 6, 0, piece, piece, beside).start()
-        copy_of(w, 7, 0, piece, at(w, 3, zo, mine), mate).start()
+        if w == 0:
+            copy_of(w, 6, k, piece, piece, beside).start()
+        copy_of(w, 5, k, piece, at(w, 3, quarter, k), mate).start()
+
+    def weight_relay(w, k):
+        m = counts[w] // 2
+        below, above = at(w, 2, zd, k), at(w, 2, zu, m + k)
+        copy_of(w, 3, k, below, below, up).wait_recv()
+        copy_of(w, 6, k, below, below, up).start()
+        copy_of(w, 4, m + k, above, above, down).wait_recv()
+        copy_of(w, 7, k, above, above, down).start()
 
     def weight_rest(w):
-        for kind, zz in ((3, zd), (4, zu)):
-            for k in range(counts[w]):
-                piece = at(w, 2, zz, k)
-                copy_of(w, kind, k, piece, piece, up).wait_recv()
-            copy_of(w, 8, kind - 3, at(w, 2, zz), at(w, 3, zz), mate).start()
-        theirs = halves(w)[1]
-        piece = at(w, 2, zo, theirs)
-        copy_of(w, 6, 0, piece, piece, beside).wait_recv()
-        copy_of(w, 8, 2, piece, at(w, 3, zo, theirs), mate).start()
+        if w == 0:
+            for j, kind, step in ((0, 3, 3), (1, 4, 1), (2, 6, 2)):
+                quarter = first_quarter(step)
+                for k in range(counts[w]):
+                    piece = at(w, 2, quarter, k)
+                    copy_of(w, kind, k, piece, piece, up).wait_recv()
+                copy_of(w, 8, j, at(w, 2, quarter), at(w, 3, quarter), mate).start()
+            return
+        m = counts[w] // 2
+        for k in range(m, 2 * m):
+            piece = at(w, 2, zd, k)
+            copy_of(w, 3, k, piece, piece, up).wait_recv()
+        copy_of(w, 8, 0, at(w, 2, zd), at(w, 3, zd), mate).start()
+        for k in range(m):
+            piece = at(w, 2, zu, k)
+            copy_of(w, 4, k, piece, piece, down).wait_recv()
+        copy_of(w, 8, 1, at(w, 2, zu), at(w, 3, zu), mate).start()
+        for k in range(m):
+            piece = at(w, 2, zo, k)
+            copy_of(w, 6, k, piece, piece, up).wait_recv()
+            piece = at(w, 2, zo, m + k)
+            copy_of(w, 7, k, piece, piece, down).wait_recv()
+        copy_of(w, 8, 2, at(w, 2, zo), at(w, 3, zo), mate).start()
 
     def weight_end(w):
-        mine, theirs = halves(w)
         own_loads[w].wait()
         copy_of(w, 0, 0, weights[w][0], at(w, 1), mate).wait_recv()
+        near, rest = (z, (zd, zu, zo)) if w else (first_quarter(0), [first_quarter(k) for k in (3, 1, 2)])
         for k in range(counts[w]):
-            copy_of(w, 5, k, at(w, 3, z, k), at(w, 3, z, k), mate).wait_recv()
-        copy_of(w, 7, 0, at(w, 3, zo, mine), at(w, 3, zo, mine), mate).wait_recv()
-        for k, zz in ((0, zd), (1, zu)):
-            copy_of(w, 8, k, at(w, 3, zz), at(w, 3, zz), mate).wait_recv()
-        copy_of(w, 8, 2, at(w, 3, zo, theirs), at(w, 3, zo, theirs), mate).wait_recv()
+            copy_of(w, 5, k, at(w, 3, near, k), at(w, 3, near, k), mate).wait_recv()
+        for k, quarter in enumerate(rest):
+            copy_of(w, 8, k, at(w, 3, quarter), at(w, 3, quarter), mate).wait_recv()
 
     def weight_sent(w):
-        piece, half, whole = at(w, 2, z, 0), at(w, 2, zo, halves(w)[0]), at(w, 2, z)
+        piece, whole = at(w, 2, z, 0), at(w, 2, z)
         copy_of(w, 0, 0, weights[w][0], at(w, 1), mate).wait_send()
-        for kind, device in ((1, cross), (3, up), (4, down), (5, mate)):
+        for kind in (1, 3, 4, 5):
             for k in range(counts[w]):
-                copy_of(w, kind, k, piece, piece, device).wait_send()
-        for kind, device in ((2, cross), (6, beside), (7, mate)):
-            copy_of(w, kind, 0, half, half, device).wait_send()
-        for k in range(2):
+                copy_of(w, kind, k, piece, piece, up).wait_send()
+        for k in range(2 if w == 0 else counts[w] // 2):
+            copy_of(w, 6, k, piece, piece, up).wait_send()
+            if w:
+                copy_of(w, 7, k, piece, piece, down).wait_send()
+        for k in range(3):
             copy_of(w, 8, k, whole, whole, mate).wait_send()
-        copy_of(w, 8, 2, half, half, mate).wait_send()
 
     pl.semaphore_wait(barrier, len(partners))
-    for w, k in CROSS:
-        if k < 0:
-            weight_cross_half(w)
-        else:
-            weight_cross(w, k)
+    for w in range(3):
+        weight_cross(w)
     for w in range(3):
         weight_near(w)
 
@@ -198,31 +209,35 @@
     m0_high = m0.astype(BF).astype(F32)
     row = iota((16, d), 0)
     shift_rows = jnp.where(row == 0, m0_high, jnp.where(row == 1, m0 - m0_high, 0.0)).astype(BF)
-    bias = jnp.sum(dot(shift_rows, wi[...]), axis=0, keepdims=True)
-
-    def fold(i, _):
+    shift[...] = shift_rows
+
+    def fold(i, total):
         rows = pl.ds(pl.multiple_of(i * 128, 128), 128)
         gain = jnp.broadcast_to(1.0 + smod[1:2, rows], (128, 128)).T
         for j in range(3):
             cols = slice(j * 128, (j + 1) * 128)
             wx[rows, cols] = (wi[rows, cols].astype(F32) * gain).astype(BF)
         wx[rows, 384:512] = jnp.ones((128, 128), BF)
-        return 0
-
-    lax.fori_loop(0, d // 128, fold, 0, unroll=4)
-    colsum = dot(jnp.ones((16, d), BF), wx[:, 0:384])[0:1, :]
+        return total + dot(shift[:, rows], wi[rows, :])
+
+    bias = lax.fori_loop(0, d // 128, fold, jnp.zeros((16, 384), F32), unroll=4)
+    bias = jnp.sum(bias, axis=0, keepdims=True)
+    tok[:, 320:336] = jnp.ones((4, 16, d), BF)
 
     def project(i, _):
-        pltpu.make_async_copy(tok_in.at[i], tok.at[i], tok_sem.at[i]).wait()
+        pltpu.make_async_copy(tok_in.at[i], tok.at[i, pl.ds(0, 320)], tok_sem.at[i]).wait()
+
+        @pl.when(i == 2)
+        def _():
+            weight_quarter(0, 0)
 
         @pl.when(i == 3)
         def _():
-            weight_quarter(0, 0)
             weight_quarter(0, 1)
-            weight_half(0)
-
-        t = tok[i]
-        raw = dot(t, wx[...])
+
+        every = dot(tok[i], wx[...])
+        raw, colsum = every[0:320], every[320:321, 0:384]
+        t = tok[i, 0:320]
         base = t[:, 0:1].astype(F32)
         squares = jnp.zeros((320, 128), F32)
         for j in range(d // 128):
@@ -263,9 +278,8 @@
     skip = first - start
     r80 = iota((80, 1), 0)
     target = ((r80 >> 1) & 7) * 32 + (r80 >> 4) * 2 + (r80 & 1) + skip
-    flat = tok.reshape(1280, d)
     windows = jnp.concatenate(
-        [flat[pl.ds(pl.multiple_of(k * 160 + start, 16), 32), :] for k in range(8)], axis=0
+        [tok[k // 2, pl.ds(pl.multiple_of((k % 2) * 160 + start, 16), 32), :] for k in range(8)], axis=0
     )
     own_rows[...] = dot(one_hot(target == iota((1, 256), 1)), windows).astype(BF)
 
@@ -391,7 +405,7 @@
         "attend": attend, "sum_begin": sum_begin, "sum_second": sum_second, "swap_send": swap_send,
         "gather_send": gather_send, "gather_relay": gather_relay, "back_second": back_second, "finish": finish,
     }
-    moves = {"temporal": temporal, "quarter": weight_quarter, "half": weight_half, "rest": weight_rest}
+    moves = {"temporal": temporal, "quarter": weight_quarter, "relay": weight_relay, "rest": weight_rest}
 
     def tick(t, _):
         for name, *what in TABLE:
@@ -456,7 +470,8 @@
         in_specs=[any_space, vmem, any_space, any_space, vmem, any_space, any_space],
         out_specs=any_space,
         scratch_shapes=[
-            pltpu.VMEM((4, 320, d), BF),
+            pltpu.VMEM((4, 336, d), BF),
+            pltpu.VMEM((16, d), BF),
             pltpu.VMEM((d, 384), BF),
             pltpu.VMEM((d, 512), BF),
             pltpu.VMEM((1280, 128), BF),

time: 89 us -> 83.9 us (0.943)
  Pallas kernels: 87 us -> 81.9 us
    pallas_call x1, Pallas kernels: 87 us -> 81.9 us  [shards(): pl.pallas_call(kernel, out_shape=jax.ShapeDtypeStruct((80, d), BF), in_sp...]
where the time goes in v4:
time: 83.9 us; the launch traced here: 83.7 us
  Pallas kernels  81.9 us (98%)
  local copies, waits for them, and re-layouts  1.84 us (2%)
    pallas_call x1, Pallas kernels, shards(): pl.pallas_call(kernel, out_shape=jax.ShapeDtypeStruct((80, d), BF), in_sp...  81.9 us
    unnamed x1, local copies, waits for them, and re-layouts  1.84 us

profile of v4, /device:TPU:0, one launch (start us, length us, event | category | flops | bytes accessed | tf_op | source)
XLA Modules:
  0.0 83.7 jit_solution(448673230105817302)
XLA Ops:
  0.0 81.9 %shard_map.73 = bf16[80,3072]{1,0:T(8,128)(2,1)} custom-call(bf16[4,320,3072]{2,1,0:T(8,128)(2,1)} %bitcast.9, f32[3,3072]{1,0:T(4,128)} %smod.1, bf16[3072,384]{1,0:T(8,128)(2,1)} %bitcast.10, bf16[4,2,16,3072]{3,2,1,0:T(8,128)(2,1)} %bitcast.12, f32[3,3072]{1,0:T(4,128)} %tmod.1, bf16[4,4,192,384]{3,2,1,0:T(8,128)(2,1)} %bitcast.11, ...), custom_call_target="tpu_custom_call" | custom-call | flops 8999999488 | bytes 16000000 | tf_op jit(solution)/shard_map/pallas_call | solution.py:467
  81.9 1.8 %copy.9 = bf16[8,10,3072]{2,0,1:T(8,128)(2,1)} copy(bf16[8,10,3072]{2,0,1:T(8,128)(2,1)} %bitcast.8) | data formatting | bytes 983040

commit v5 on v4

--- a/solution.py
+++ b/solution.py
@@ -26,6 +26,7 @@
     ("temporal", 15, 2, 4),
     ("temporal", 17, 4, 5),
     ("back_second", (15, 0), (16, 1), (17, 2), (18, 3), (19, 4)),
+    ("drain", 19),
     ("finish", (17, 0), (18, 1), (19, 2), (20, 3), (21, 4)),
     ("quarter", 0, 1, 0),
     ("quarter", 2, 1, 1),
@@ -67,7 +68,7 @@
     tok_in, smod, win_in, wo_in, tmod, wt_in, wto_in,
     out,
     tok, shift, wi, wx, qb, kb, vx, att, cat, own_rows, wo, wt, wto,
-    part, relay, got, shuf, shufr, gath, part2, relay2, got2, res,
+    part, relay, got, shuf, shufr, gath, tnorm, part2, relay2, got2, res,
     local_sem, tok_sem, out_sem, win_sem, wsend, wrecv, asend, arecv,
     rsend, rrecv, ssend, srecv, gsend, grecv, rsend2, rrecv2,
 ):
@@ -289,11 +290,13 @@
     from_recv = one_hot((r128 & 7) * 16 + ((r128 >> 3) & 1) * 8 + (r128 >> 4) == c128)
     lo, hi = pl.ds(0, hb), pl.ds(hb, hb)
 
-    def ring_first(b, buf, rel, rec, ss, rs):
-        remote(buf.at[b, xo, :, lo], rel.at[b, 0], ss.at[b, 0], rs.at[b, 0], right).start()
-        remote(buf.at[b, xo, :, hi], rel.at[b, 1], ss.at[b, 1], rs.at[b, 1], left).start()
-        remote(buf.at[b, xr, :, hi], rec.at[b, 0, 1], ss.at[b, 2], rs.at[b, 2], right).start()
-        remote(buf.at[b, xl, :, lo], rec.at[b, 1, 0], ss.at[b, 3], rs.at[b, 3], left).start()
+    def ring_first(b, half, buf, rel, rec, ss, rs):
+        if half == 0:
+            remote(buf.at[b, xo, :, lo], rel.at[b, 0], ss.at[b, 0], rs.at[b, 0], right).start()
+            remote(buf.at[b, xl, :, lo], rec.at[b, 1, 0], ss.at[b, 3], rs.at[b, 3], left).start()
+        else:
+            remote(buf.at[b, xo, :, hi], rel.at[b, 1], ss.at[b, 1], rs.at[b, 1], left).start()
+            remote(buf.at[b, xr, :, hi], rec.at[b, 0, 1], ss.at[b, 2], rs.at[b, 2], right).start()
 
     def ring_second(b, buf, rel, rec, ss, rs):
         remote(rel.at[b, 0], rel.at[b, 0], ss.at[b, 0], rs.at[b, 0], right).wait_recv()
@@ -326,8 +329,9 @@
         for r in (1, 2, 3):
             remote(cat.at[b, r], cat.at[b, r], asend.at[b, r], arecv.at[b, r], quad[r]).wait_recv()
         lhs = jnp.concatenate([att[b, q], cat[b, 1], cat[b, 2], cat[b, 3]], axis=1)
-        part[b] = dot(lhs, wo[...].reshape(512, d)).astype(BF).reshape(4, 16, d)
-        ring_first(b, part, relay, got, rsend, rrecv)
+        for half, cols in ((0, lo), (1, hi)):
+            part[b, :, :, cols] = dot(lhs, wo[:, :, :, :, cols].reshape(512, hb)).astype(BF).reshape(4, 16, hb)
+            ring_first(b, half, part, relay, got, rsend, rrecv)
 
     def swap_send(b):
         total = ring_last(b, part, got, rsend, rrecv)
@@ -335,7 +339,7 @@
         middle = (rows.astype(F32) + smod[2:3, :] * total).astype(BF)
         stacked = jnp.concatenate([middle[:, k * eighth:(k + 1) * eighth] for k in range(8)], axis=0)
         shuf[b] = dot(to_send, stacked).astype(BF).reshape(8, 16, eighth)
-        for j in (4, 1, 7, 5, 3, 2, 6):
+        for j in (2, 6, 3, 5, 1, 7, 4):
             to = (s + j) % 8
             remote(shuf.at[b, to], shufr.at[b, s], ssend.at[b, j], srecv.at[b, j], (to, h)).start()
         shufr[b, s] = shuf[b, s]
@@ -365,14 +369,23 @@
             far = gath.at[b, xo]
             remote(far.at[:, lo], far.at[:, lo], gsend.at[b, 2], grecv.at[b, 2], right).wait_recv()
             remote(far.at[:, hi], far.at[:, hi], gsend.at[b, 3], grecv.at[b, 3], left).wait_recv()
-        rows = gath[lead:last].reshape(n, d).astype(F32)
-        center = rows - jnp.sum(rows, axis=1, keepdims=True) * (1.0 / d)
-        spread = jnp.sum(center * center, axis=1, keepdims=True) * (1.0 / d)
+        rows = gath[lead:last].reshape(n, d)
+        base = rows[:, 0:1].astype(F32)
+        total, squares = jnp.zeros((n, 128), F32), jnp.zeros((n, 128), F32)
+        for k in range(d // 128):
+            e = rows[:, k * 128:(k + 1) * 128].astype(F32) - base
+            total, squares = total + e, squares + e * e
+        off = jnp.sum(total, axis=1, keepdims=True) * (1.0 / d)
+        spread = jnp.sum(squares, axis=1, keepdims=True) * (1.0 / d) - off * off
         scale = lax.rsqrt(spread + 1e-06)
-        normed = (center * scale * (1.0 + tmod[1:2, :]) + tmod[0:1, :]).astype(BF)
+        mean = base + off
+        for k in range(d // 128):
+            cols = slice(k * 128, (k + 1) * 128)
+            center = (rows[:, cols].astype(F32) - mean) * scale
+            tnorm[0:n, cols] = (center * (1.0 + tmod[1:2, cols]) + tmod[0:1, cols]).astype(BF)
         if lead == 0:
             weight_end(1)
-        joined = dot(normed, wt[...].reshape(d, 1536)).astype(BF)
+        joined = dot(tnorm[0:n], wt[...].reshape(d, 1536)).astype(BF)
         same = (iota((n, n), 0) >> 3) == (iota((n, n), 1) >> 3)
         attended = []
         for j in range(4):
@@ -385,9 +398,11 @@
         if lead == 0:
             weight_end(2)
         lhs = jnp.concatenate(attended, axis=1)
-        part2[lead:last] = dot(lhs, wto[...].reshape(512, d)).astype(BF).reshape(last - lead, 4, 16, d)
-        for b in range(lead, last):
-            ring_first(b, part2, relay2, got2, rsend2, rrecv2)
+        for half, cols in ((0, lo), (1, hi)):
+            some = dot(lhs, wto[:, :, :, :, cols].reshape(512, hb)).astype(BF)
+            part2[lead:last, :, :, cols] = some.reshape(last - lead, 4, 16, hb)
+            for b in range(lead, last):
+                ring_first(b, half, part2, relay2, got2, rsend2, rrecv2)
 
     def back_second(b):
         ring_second(b, part2, relay2, got2, rsend2, rrecv2)
@@ -401,11 +416,29 @@
     def sum_second(b):
         ring_second(b, part, relay, got, rsend, rrecv)
 
+    def sent(b, _):
+        for r in (1, 2, 3):
+            remote(cat.at[b, r], cat.at[b, r], asend.at[b, r], arecv.at[b, r], quad[r]).wait_send()
+        ring_sent(b, relay, rsend, rrecv)
+        for j in range(1, 8):
+            piece = shuf.at[b, 0]
+            remote(piece, piece, ssend.at[b, j], srecv.at[b, j], right).wait_send()
+        for k in range(4):
+            piece = gath.at[b, x] if k < 2 else gath.at[b, x, :, lo]
+            remote(piece, piece, gsend.at[b, k], grecv.at[b, k], right).wait_send()
+        return 0
+
+    def drain():
+        lax.fori_loop(0, nb, sent, 0)
+        for w in range(3):
+            weight_sent(w)
+
     blocks = {
         "attend": attend, "sum_begin": sum_begin, "sum_second": sum_second, "swap_send": swap_send,
         "gather_send": gather_send, "gather_relay": gather_relay, "back_second": back_second, "finish": finish,
     }
-    moves = {"temporal": temporal, "quarter": weight_quarter, "relay": weight_relay, "rest": weight_rest}
+    moves = {"temporal": temporal, "quarter": weight_quarter, "relay": weight_relay, "rest": weight_rest,
+        "drain": drain}
 
     def tick(t, _):
         for name, *what in TABLE:
@@ -430,22 +463,11 @@
     for b in range(nb):
         pltpu.make_async_copy(res.at[b], out.at[pl.ds(b * 16, 16), :], out_sem.at[b]).wait()
 
-    def sent(b, _):
-        for r in (1, 2, 3):
-            remote(cat.at[b, r], cat.at[b, r], asend.at[b, r], arecv.at[b, r], quad[r]).wait_send()
-        ring_sent(b, relay, rsend, rrecv)
+    def back_sent(b, _):
         ring_sent(b, relay2, rsend2, rrecv2)
-        for j in range(1, 8):
-            piece = shuf.at[b, 0]
-            remote(piece, piece, ssend.at[b, j], srecv.at[b, j], right).wait_send()
-        for k in range(4):
-            piece = gath.at[b, x] if k < 2 else gath.at[b, x, :, lo]
-            remote(piece, piece, gsend.at[b, k], grecv.at[b, k], right).wait_send()
         return 0
 
-    lax.fori_loop(0, nb, sent, 0)
-    for w in range(3):
-        weight_sent(w)
+    lax.fori_loop(0, nb, back_sent, 0)
 
 
 def shards(
@@ -487,6 +509,7 @@
             pltpu.VMEM((nb, 8, 16, d // 8), BF),
             pltpu.VMEM((nb, 8, 16, d // 8), BF),
             pltpu.VMEM((nb, 4, 16, d), BF),
+            pltpu.VMEM((nb * 64, d), BF),
             *ring,
             pltpu.VMEM((nb, 16, d), BF),
             dma((3,)), dma((4,)), dma((nb,)), dma(()),

time: 83.9 us -> 83.7 us (level)
  no operation moved by 1% of the time
where the time goes in v5:
time: 83.7 us; the launch traced here: 83.4 us
  Pallas kernels  81.5 us (97%)
  local copies, waits for them, and re-layouts  1.84 us (2%)
    pallas_call x1, Pallas kernels, shards(): pl.pallas_call(kernel, out_shape=jax.ShapeDtypeStruct((80, d), BF), in_sp...  81.5 us
    unnamed x1, local copies, waits for them, and re-layouts  1.84 us

profile of v5, /device:TPU:0, one launch (start us, length us, event | category | flops | bytes accessed | tf_op | source)
XLA Modules:
  0.0 83.4 jit_solution(3077022117791779423)
XLA Ops:
  0.0 81.5 %shard_map.73 = bf16[80,3072]{1,0:T(8,128)(2,1)} custom-call(bf16[4,320,3072]{2,1,0:T(8,128)(2,1)} %bitcast.9, f32[3,3072]{1,0:T(4,128)} %smod.1, bf16[3072,384]{1,0:T(8,128)(2,1)} %bitcast.10, bf16[4,2,16,3072]{3,2,1,0:T(8,128)(2,1)} %bitcast.12, f32[3,3072]{1,0:T(4,128)} %tmod.1, bf16[4,4,192,384]{3,2,1,0:T(8,128)(2,1)} %bitcast.11, ...), custom_call_target="tpu_custom_call" | custom-call | flops 8999999488 | bytes 16000000 | tf_op jit(solution)/shard_map/pallas_call | solution.py:489
  81.6 1.8 %copy.9 = bf16[8,10,3072]{2,0,1:T(8,128)(2,1)} copy(bf16[8,10,3072]{2,0,1:T(8,128)(2,1)} %bitcast.8) | data formatting | bytes 983040

commit v6 on v5

--- a/solution.py
+++ b/solution.py
@@ -108,8 +108,7 @@
         pltpu.make_async_copy(wt_in, wt.at[:, :, :, pl.ds(0, 384)], local_sem.at[1]),
         pltpu.make_async_copy(wto_in, wto.at[0], local_sem.at[2]),
     ]
-    for load in own_loads:
-        load.start()
+    own_loads[0].start()
 
     counts = (2, 4, 2)
 
@@ -202,8 +201,7 @@
     pl.semaphore_wait(barrier, len(partners))
     for w in range(3):
         weight_cross(w)
-    for w in range(3):
-        weight_near(w)
+    weight_near(0)
 
     load_w.wait()
     m0 = smod[0:1, :]
@@ -256,6 +254,9 @@
         return 0
 
     lax.fori_loop(0, 4, project, 0)
+    for w in (1, 2):
+        own_loads[w].start()
+        weight_near(w)
 
     score_scale = 128 ** (-0.5) * LOG2E
 

time: 83.7 us -> 83.5 us (level)
  no operation moved by 1% of the time
where the time goes in v6:
time: 83.5 us; the launch traced here: 83.3 us
  Pallas kernels  81.4 us (97%)
  local copies, waits for them, and re-layouts  1.84 us (2%)
    pallas_call x1, Pallas kernels, shards(): pl.pallas_call(kernel, out_shape=jax.ShapeDtypeStruct((80, d), BF), in_sp...  81.4 us
    unnamed x1, local copies, waits for them, and re-layouts  1.84 us

profile of v6, /device:TPU:0, one launch (start us, length us, event | category | flops | bytes accessed | tf_op | source)
XLA Modules:
  0.0 83.3 jit_solution(10305143700445457910)
XLA Ops:
  0.0 81.4 %shard_map.73 = bf16[80,3072]{1,0:T(8,128)(2,1)} custom-call(bf16[4,320,3072]{2,1,0:T(8,128)(2,1)} %bitcast.9, f32[3,3072]{1,0:T(4,128)} %smod.1, bf16[3072,384]{1,0:T(8,128)(2,1)} %bitcast.10, bf16[4,2,16,3072]{3,2,1,0:T(8,128)(2,1)} %bitcast.12, f32[3,3072]{1,0:T(4,128)} %tmod.1, bf16[4,4,192,384]{3,2,1,0:T(8,128)(2,1)} %bitcast.11, ...), custom_call_target="tpu_custom_call" | custom-call | flops 8999999488 | bytes 16000000 | tf_op jit(solution)/shard_map/pallas_call | solution.py:490
  81.4 1.8 %copy.9 = bf16[8,10,3072]{2,0,1:T(8,128)(2,1)} copy(bf16[8,10,3072]{2,0,1:T(8,128)(2,1)} %bitcast.8) | data formatting | bytes 983040
